TPU v7x, 128 devices: a whole 4x4x4 slice. The times are simulated.
128 devices in a mesh: var: 4 (over z), patch: 32 (over x, y, core).
Axes of the slice: x: 4, y: 4, z: 4, core: 2. Of those that a mesh axis runs over, the one named last changes fastest.
Arguments:
- tokens: bfloat16 [48, 16384, 1024], P('var', 'patch'), may hold values from -8.25 to 8.25
- key_query: bfloat16 [1024, 16], replicated, may hold values from -0.2 to 0.2
- value_weight: bfloat16 [1024, 1024], replicated, may hold values from -0.1875 to 0.1875
- proj_weight: bfloat16 [1024, 2048], replicated, may hold values from -0.1875 to 0.1875
- norm_gain: float32 [2048], replicated, may hold values from 0.1 to 1.9
- qkv_weight: bfloat16 [2048, 3, 16, 128], P(None, None, 'var'), may hold values from -0.3 to 0.3
- out_weight: bfloat16 [16, 128, 2048], P('var'), may hold values from -0.125 to 0.125
Outputs:
- block_out: bfloat16 [16384, 2048], P('patch', 'var')
All inputs are finite; a program needn't handle non-finite values.
Results may differ from a plain program's by a relative error of at most 0.006.
Values may be sent and summed in bfloat16 or wider, within the bound.
A program may use at most 192 MiB of HBM per device.

v0:
```python
import math

import jax
import jax.numpy as jnp
from jax import lax
from jax.sharding import PartitionSpec as P


def make_folder(queries):

    def fold_keys(carry, pieces, start):
        key_piece, value_piece = pieces
        count = key_piece.shape[0]
        block_len = math.gcd(count, 1024)
        key_blocks = key_piece.reshape((count // block_len, block_len) + key_piece.shape[1:])
        value_blocks = value_piece.reshape((count // block_len, block_len) + value_piece.shape[1:])

        def one_block(state, blocks):
            running_max, running_sum, running_acc = state
            key_block, value_block = blocks
            logits = jnp.einsum(
                "qhd,khd->hqk", queries, key_block, preferred_element_type=jnp.float32
            )
            new_max = jnp.maximum(running_max, jnp.max(logits, axis=2))
            rescale = jnp.exp(running_max - new_max)
            expw = jnp.exp(logits - new_max[..., None])
            new_sum = running_sum * rescale + jnp.sum(expw, axis=2)
            contrib = jnp.einsum(
                "hqk,khd->hqd",
                expw.astype(jnp.bfloat16),
                value_block,
                preferred_element_type=jnp.float32,
            )
            return ((new_max, new_sum, running_acc * rescale[..., None] + contrib), None)

        state, _ = lax.scan(one_block, carry, (key_blocks, value_blocks))
        return state

    return fold_keys


def on_device(tokens, key_query, value_weight, proj_weight, norm_gain, qkv_weight, out_weight):
    dim = tokens.shape[2]
    heads = key_query.shape[1]
    rows = tokens.shape[1]
    scores = jnp.einsum("vpd,dh->vph", tokens, key_query, preferred_element_type=jnp.float32)
    peak = jnp.max(scores, axis=0)
    weights = jnp.exp(scores - peak[None])
    totals = jnp.sum(weights, axis=0)
    rounded = weights.astype(jnp.bfloat16)
    mixture = jnp.einsum(
        "vph,vpd->phd", rounded, tokens, preferred_element_type=jnp.float32
    ).astype(jnp.bfloat16)
    heads_weight = value_weight.reshape(dim, heads, dim // heads)
    partial_sums = jnp.einsum(
        "phd,dhj->phj", mixture, heads_weight, preferred_element_type=jnp.float32
    ).reshape(rows, dim)
    highest = lax.pmax(peak.astype(jnp.bfloat16), "var").astype(peak.dtype)
    factor = jnp.exp(peak - highest)
    scaled = (partial_sums.reshape(rows, heads, -1) * factor[..., None]).reshape(rows, dim)
    denom, numer = lax.psum((totals * factor, scaled), "var")
    pooled = (
        (numer.reshape(rows, heads, -1) / denom[..., None]).reshape(rows, dim).astype(jnp.bfloat16)
    )
    embedded = jnp.dot(pooled, proj_weight, preferred_element_type=jnp.float32)
    center = embedded - jnp.mean(embedded, axis=1, keepdims=True)
    variance = jnp.mean(center * center, axis=1, keepdims=True)
    normed = (center / jnp.sqrt(variance + 1e-05) * norm_gain).astype(jnp.bfloat16)
    width = normed.shape[1]
    local_heads = qkv_weight.shape[2]
    head_size = qkv_weight.shape[3]
    projected = jnp.dot(
        normed,
        qkv_weight.reshape(width, 3 * local_heads * head_size),
        preferred_element_type=jnp.float32,
    )
    projected = projected.reshape(rows, 3, local_heads, head_size)
    queries = (projected[:, 0] * head_size ** (-0.5)).astype(jnp.bfloat16)
    keys = projected[:, 1].astype(jnp.bfloat16)
    values = projected[:, 2].astype(jnp.bfloat16)
    start_state = (
        jnp.full((local_heads, rows), -1e30, jnp.float32),
        jnp.zeros((local_heads, rows), jnp.float32),
        jnp.zeros((local_heads, rows, head_size), jnp.float32),
    )
    fold_keys = make_folder(queries)
    all_keys, all_values = (
        lax.all_gather(keys, "patch", axis=0, tiled=True),
        lax.all_gather(values, "patch", axis=0, tiled=True),
    )
    final_state = fold_keys(start_state, (all_keys, all_values), 0)
    running_max, running_sum, running_acc = final_state
    attended = running_acc / running_sum[..., None]
    attended = (
        jnp.transpose(attended, (1, 0, 2))
        .reshape(rows, local_heads * head_size)
        .astype(jnp.bfloat16)
    )
    branch = jnp.dot(
        attended,
        out_weight.reshape(local_heads * head_size, width),
        preferred_element_type=jnp.float32,
    )
    reduced = lax.psum_scatter(branch, "var", scatter_dimension=1, tiled=True)
    share = reduced.shape[1]
    residual = lax.dynamic_slice_in_dim(embedded, lax.axis_index("var") * share, share, 1)
    return (residual + reduced).astype(jnp.bfloat16)


def solution(mesh):
    return jax.shard_map(
        on_device,
        mesh=mesh,
        in_specs=(
            P("var", "patch", None),
            P(),
            P(),
            P(),
            P(),
            P(None, None, "var", None),
            P("var", None, None),
        ),
        out_specs=P("patch", "var"),
        check_vma=False,
    )
```

profile of v0, /device:TPU:0, one launch (start us, length us, event | category | flops | bytes accessed | tf_op | source)
XLA Modules:
  0.0 591.6 jit_solution(1134463523628077880)
XLA Ops:
  6.5 8.1 %fusion.34 = (f32[512,16]{0,1:T(8,128)S(1)}, f32[12,512,16]{1,2,0:T(8,128)S(1)}) fusion(bf16[12,512,1024]{2,1,0:T(8,128)(2,1)} %param.9, bf16[1024,16]{0,1:T(8,128)(2,1)} %param.10), kind=kOutput, calls=%fused_computation.50 | convolution fusion | flops 201416704 | bytes 13041664 | tf_op jit(solution)/shard_map/vpd,dh->vph/dot_general | solution.py:46
  14.7 18.3 %pmax.7 = bf16[512,16]{0,1:T(8,128)(2,1)S(1)} all-reduce(bf16[512,16]{0,1:T(8,128)(2,1)S(1)} %convert_element_type.47), channel_id=1, replica_groups=mesh['var'=4,'patch'=32] {'var'}, use_global_device_ids=true, to_apply=%region_1.0 | all-reduce | flops 8192 | bytes 32768 | tf_op jit(solution)/shard_map/pmax | solution.py:58
  35.8 18.8 %fusion.18 = bf16[512,16,1024]{2,1,0:T(8,128)(2,1)} fusion(bf16[12,512,16]{2,0,1:T(8,128)(2,1)} %copy.19, bf16[12,512,1024]{2,1,0:T(8,128)(2,1)} %param.9), kind=kOutput, calls=%fused_computation.22 | convolution fusion | flops 201326592 | bytes 29556736 | tf_op jit(solution)/shard_map/vph,vpd->phd/dot_general | solution.py:51
  58.6 18.7 %bitcast_multiply_fusion = f32[512,16,64]{0,2,1:T(8,128)} fusion(bf16[1024,16,64]{0,2,1:T(8,128)(2,1)} %bitcast.80, bf16[512,16,1024]{2,1,0:T(8,128)(2,1)} %fusion.18, f32[512,16]{0,1:T(8,128)S(1)} %get-tuple-element.100), kind=kOutput, calls=%fused_computation.31 | convolution fusion | flops 1074266112 | bytes 21004288 | tf_op jit(solution)/shard_map/phd,dhj->phj/dot_general | solution.py:55
  77.4 11.1 %reshape.49 = bf16[2048,1536]{1,0:T(8,128)(2,1)} reshape(bf16[2048,3,4,128]{3,2,1,0:T(4,128)(2,1)} %param.14) | data formatting | bytes 12582912 | tf_op jit(solution)/shard_map/reshape | solution.py:74
  88.5 8.7 %copy.15 = bf16[1536,2048]{1,0:T(8,128)(2,1)} copy(bf16[1536,2048]{0,1:T(8,128)(2,1)} %bitcast.75) | data formatting | bytes 12582912 | tf_op jit(solution)/shard_map/dot_general | solution.py:72
  97.2 14.6 %psum.15 = f32[512,16]{0,1:T(8,128)S(1)} all-reduce(f32[512,16]{0,1:T(8,128)S(1)} %get-tuple-element.99), channel_id=1, replica_groups=mesh['var'=4,'patch'=32] {'var'}, use_global_device_ids=true, to_apply=%region_4.0 | all-reduce | flops 8192 | bytes 65536 | tf_op jit(solution)/shard_map/psum | solution.py:61
  111.9 24.1 %all-reduce.2.cloned.1.call-done = f32[512,1024]{0,1:T(8,128)} async-done(((f32[512,1024]{0,1:T(8,128)}), f32[512,1024]{0,1:T(8,128)}) %all-reduce.2.cloned.1.call-update) | async-done | bytes 2097168 | tf_op jit(solution)/shard_map/psum | solution.py:61
  138.0 4.9 fusion.35
  143.5 5.2 fusion.36
  152.8 69.2 %all-gather.7.cloned.1.call-done = bf16[16384,1,4,128]{3,0,2,1:T(8,128)(2,1)} async-done(((bf16[512,1,4,128]{3,0,2,1:T(8,128)(2,1)}), bf16[16384,1,4,128]{3,0,2,1:T(8,128)(2,1)}) %all-gather.7.cloned.1.call-update) | async-done | bytes 16777232 | tf_op jit(solution)/shard_map/all_gather | solution.py:89
  222.0 74.6 %all-gather.5.cloned.1.call-done = bf16[16384,1,4,128]{3,0,2,1:T(8,128)(2,1)} async-done(((bf16[512,1,4,128]{3,0,2,1:T(8,128)(2,1)}), bf16[16384,1,4,128]{3,0,2,1:T(8,128)(2,1)}) %all-gather.5.cloned.1.call-update) | async-done | bytes 16777232 | tf_op jit(solution)/shard_map/all_gather | solution.py:88
  296.5 236.0 %while.15 = (s32[]{:T(128)}, f32[4,512]{1,0:T(4,128)S(1)}, f32[4,512]{1,0:T(4,128)S(1)}, f32[4,512,128]{2,1,0:T(8,128)S(1)}, bf16[16,1024,4,128]{3,1,0,2:T(8,128...) while((s32[]{:T(128)}, f32[4,512]{1,0:T(4,128)S(1)}, ...), condition=%wide.region_10.11_spmd.clone, body=%wide.region_7.10_spmd.clone.sunk | while | flops 1085024256 | bytes 63571076 | solution.py:36
  296.5 5.8 bitcast_reduce_fusion.2
  311.3 5.8 bitcast_reduce_fusion.2
  326.0 5.8 bitcast_reduce_fusion.2
  340.8 5.8 bitcast_reduce_fusion.2
  355.5 5.8 bitcast_reduce_fusion.2
  370.3 5.8 bitcast_reduce_fusion.2
  385.0 5.8 bitcast_reduce_fusion.2
  399.8 5.8 bitcast_reduce_fusion.2
  405.6 4.7 fusion.54
  414.5 5.8 bitcast_reduce_fusion.2
  429.3 5.8 bitcast_reduce_fusion.2
  444.0 5.8 bitcast_reduce_fusion.2
  458.8 5.8 bitcast_reduce_fusion.2
  473.6 5.8 bitcast_reduce_fusion.2
  488.3 5.8 bitcast_reduce_fusion.2
  503.1 5.8 bitcast_reduce_fusion.2
  508.9 4.7 fusion.54
  517.8 5.8 bitcast_reduce_fusion.2
  535.8 46.7 %reduce-scatter.2.cloned.1.call-done = f32[512,512]{1,0:T(8,128)} async-done(((f32[512,2048]{1,0:T(8,128)}), f32[512,512]{1,0:T(8,128)}) %reduce-scatter.2.cloned.1.call-update) | async-done | bytes 1048592 | tf_op jit(solution)/shard_map/reduce_scatter | solution.py:104
  (145 shorter events, 152.1 us)
Async XLA Ops:
  6.5 526.0 %copy-start = (bf16[4,128,2048]{2,1,0:T(8,128)(2,1)S(1)}, bf16[4,128,2048]{2,1,0:T(8,128)(2,1)}, u32[]{:S(2)}) copy-start(bf16[4,128,2048]{2,1,0:T(8,128)(2,1)} %param.15) | copy-start | bytes 6291460
  6.5 129.4 %all-reduce.2.cloned.1.call-start = ((), (), s32[]{:S(2)}) async-start(), calls=%async_computation.1 | async-start | bytes 4194304 | tf_op jit(solution)/shard_map/psum | solution.py:61
  77.3 144.6 %all-gather.7.cloned.1.call-start = ((), (), s32[]{:S(2)}) async-start(), calls=%async_computation.4 | async-start | bytes 17301504 | tf_op jit(solution)/shard_map/all_gather | solution.py:89
  136.0 7.5 %slice-start = ((s8[6291456]{0:T(1024)(128)(4,1)}), s8[4194304]{0:T(1024)(128)(4,1)S(1)}, s32[]{:S(2)}) async-start(s8[6291456]{0:T(1024)(128)(4,1)} %bitcast.76), calls=%async_computation.5 | async-start | bytes 8388608
  138.0 5.5 slice-start.1
  142.8 5.9 %copy-start.2 = (f32[512,2048]{1,0:T(8,128)}, f32[512,2048]{1,0:T(8,128)S(1)}, u32[]{:S(2)}) copy-start(f32[512,2048]{1,0:T(8,128)S(1)} %get-tuple-element.110) | copy-start | bytes 12582916
  142.8 0.7 copy-start.3
  149.8 146.7 %all-gather.5.cloned.1.call-start = ((), (), s32[]{:S(2)}) async-start(), calls=%async_computation.3 | async-start | bytes 17301504 | tf_op jit(solution)/shard_map/all_gather | solution.py:88
  150.6 432.0 %reduce-scatter.2.cloned.1.call-start = ((), (), s32[]{:S(2)}) async-start(), calls=%async_computation.2 | async-start | bytes 5242880 | tf_op jit(solution)/shard_map/reduce_scatter | solution.py:104
  302.4 5.8 copy-start.1
  317.1 5.8 copy-start.1
  331.9 5.8 copy-start.1
  346.6 5.8 copy-start.1
  361.4 5.8 copy-start.1
  376.1 5.8 copy-start.1
  390.9 5.8 copy-start.1
  405.6 5.8 copy-start.1
  420.4 5.8 copy-start.1
  435.1 5.8 copy-start.1
  449.9 5.8 copy-start.1
  464.6 5.8 copy-start.1
  479.4 5.8 copy-start.1
  494.1 5.8 copy-start.1
  508.9 5.8 copy-start.1
  523.6 5.8 copy-start.1
Sparse Core Ops, SparseCore 0:
  77.5 58.4 all-reduce.1
  149.9 71.9 all-gather.6
  224.6 71.8 all-gather.4
  536.0 46.5 reduce-scatter.1
where the time goes:
time: 594 us; the launch traced here: 592 us
  waiting for transfers between devices  215 us (36%)
  matrix products  202 us (34%)
  other arithmetic  82.9 us (14%)
  local copies, waits for them, and re-layouts  44.4 us (7%)
  blocking collectives  32.9 us (6%)
  between operations  13.3 us (2%)
    dot_general x16, matrix products, one_block(): jnp.einsum('qhd,khd->hqk', queries, key_block, preferred_element_type=jnp...  93.1 us
    reduce_sum x16, other arithmetic, one_block(): new_sum = running_sum * rescale + jnp.sum(expw, axis=2)  75.2 us
    all_gather x1, waiting for transfers between devices, on_device(): lax.all_gather(keys, 'patch', axis=0, tiled=True)  74.6 us
    all_gather x1, waiting for transfers between devices, on_device(): lax.all_gather(values, 'patch', axis=0, tiled=True)  69.2 us
    dot_general x16, matrix products, one_block(): jnp.einsum('hqk,khd->hqd', expw.astype(jnp.bfloat16), value_block, prefer...  49.9 us
    reduce_scatter x1, waiting for transfers between devices, on_device(): reduced = lax.psum_scatter(branch, 'var', scatter_dimension=1, tiled=True)  46.7 us
    psum x1, waiting for transfers between devices, on_device(): denom, numer = lax.psum((totals * factor, scaled), 'var')  24.1 us
    dot_general x1, matrix products, on_device(): jnp.einsum('vph,vpd->phd', rounded, tokens, preferred_element_type=jnp.fl...  18.8 us
  transfers between devices with their start and end apart: 4, of which 4 were waited for; matrix products, arithmetic and copies ran while one was open for 4% of the time, Pallas kernels for 0%

commit v1 on v0

v1 whole, which is shorter than its diff:
```python
import functools

import jax
import jax.numpy as jnp
from jax import lax
from jax.experimental import pallas as pl
from jax.experimental.pallas import tpu as pltpu
from jax.sharding import PartitionSpec as P

MESH = pl.DeviceIdType.MESH
NT = (((1,), (1,)), ((), ()))
BF = jnp.bfloat16
F32 = jnp.float32

ROWS, NV, CH = 512, 12, 128
Q_SCALE = 128 ** (-0.5) * 1.4426950408889634


def order(e):
    if isinstance(e, int):
        return (0, 1, 3, 2)[e]
    return e + lax.div(e, 2) * (5 - 2 * e)


def dot(a, b):
    return jnp.dot(a, b, preferred_element_type=F32)


def kernel(
    tok_hbm, kq_ref, vw_hbm, proj_hbm, gain_ref, w2_hbm, ow_hbm,
    out_ref,
    tok, kqp, expand, vw, proj, wstage, wf, wq,
    wn, part_send, part_recv, stat_send, stat_recv, pooled,
    emb, normed, q4, kv4, q_buf, kv, s0, s1, acc, mref,
    ow, stage, att,
    sem_tok, sem_w, sem_w2, sem_ow_own,
    ps_send, ps_recv, st_send, st_recv, pool_send, pool_recv,
    q_send, q_recv, kvx_send, own_send, fwd_send, kv_recv,
    ow_send, ow_recv, ax_send, ax_recv, az_send, az_recv,
):
    z = lax.axis_index("var")
    place = lax.axis_index("patch")
    x = lax.div(place, 8)
    y = lax.rem(lax.div(place, 2), 4)
    c = lax.rem(place, 2)

    def at(dx=0, dy=0, dz=0, dc=0):
        px = lax.rem(x + dx, 4)
        py = lax.rem(y + dy, 4)
        pc = lax.rem(c + dc, 2)
        return (lax.rem(z + dz, 4), (px * 4 + py) * 2 + pc)

    def remote(src, dst, send, recv, device):
        return pltpu.make_async_remote_copy(
            src_ref=src, dst_ref=dst, send_sem=send, recv_sem=recv,
            device_id=device, device_id_type=MESH,
        )

    def tok_copy(j, slot):
        base = pl.multiple_of(lax.rem(z + order(3 - j), 4) * CH, CH)
        return pltpu.make_async_copy(
            tok_hbm.at[:, pl.ds(base, CH), :], tok.at[slot], sem_tok.at[slot]
        )

    vw_copy = pltpu.make_async_copy(vw_hbm, vw, sem_w.at[0])
    proj_copy = pltpu.make_async_copy(proj_hbm, proj, sem_w.at[1])
    tok_copy(0, 0).start()
    vw_copy.start()
    tok_copy(1, 1).start()
    proj_copy.start()

    def w2_copy(i, slot):
        base = pl.multiple_of(i * 1536, 1536)
        return pltpu.make_async_copy(
            w2_hbm.at[pl.ds(base, 1536), :], wstage.at[slot], sem_w2.at[slot]
        )

    w2_copy(0, 0).start()
    w2_copy(1, 1).start()

    barrier = pltpu.get_barrier_semaphore()
    partners = [at(dx=d) for d in (1, 2, 3)] + [at(dy=d) for d in (1, 2, 3)]
    partners += [at(dz=d) for d in (1, 2, 3)] + [at(dc=1)]
    for device in partners:
        pl.semaphore_signal(barrier, inc=1, device_id=device, device_id_type=MESH)
    pl.semaphore_wait(barrier, len(partners))

    kqp[...] = jnp.zeros_like(kqp)
    kqp[0:16, :] = kq_ref[...]
    head_of = lax.broadcasted_iota(jnp.int32, (128, 1024), 0)
    lane = lax.broadcasted_iota(jnp.int32, (128, 1024), 1)
    expand[...] = jnp.where(lax.div(lane, 64) == head_of, 1.0, 0.0).astype(BF)

    vw_copy.wait()

    def part_copy(j):
        dz = order(3 - j)
        return remote(
            part_send.at[j], part_recv.at[3 - dz], ps_send.at[j], ps_recv.at[3 - dz], at(dz=dz)
        )

    def stat_copy(j):
        dz = order(3 - j)
        return remote(
            stat_send.at[j], stat_recv.at[3 - dz], st_send.at[j], st_recv.at[3 - dz], at(dz=dz)
        )

    def pool_chunk(j, _):
        slot = lax.rem(j, 2)
        tok_copy(j, slot).wait()
        scores = lax.dot_general(
            tok[slot].reshape(NV * CH, 1024), kqp[...], NT, preferred_element_type=F32
        ).reshape(NV, CH, 128)
        peak = jnp.max(scores, axis=0)
        weights = jnp.exp(scores - peak[None])
        totals = jnp.sum(weights, axis=0)
        first_lanes = lax.broadcasted_iota(jnp.int32, (CH, 128), 1) < 16
        stat_send[j] = jnp.where(first_lanes, peak, pltpu.roll(totals, 16, 1))
        wn[...] = weights.astype(BF).reshape(NV * CH, 128)

        def columns(i, _):
            cs = pl.ds(pl.multiple_of(i * 256, 256), 256)
            values = dot(tok[slot].reshape(NV * CH, 1024), vw[:, cs])
            wide = dot(wn[...], expand[:, cs])
            summed = jnp.sum((values * wide).reshape(NV, CH, 256), axis=0)
            part_send[j, :, cs] = summed.astype(BF)
            return 0

        lax.fori_loop(0, 4, columns, 0)

        @pl.when(j < 2)
        def _():
            tok_copy(j + 2, slot).start()

        @pl.when(j < 3)
        def _():
            part_copy(j).start()
            stat_copy(j).start()

        return 0

    lax.fori_loop(0, 4, pool_chunk, 0)

    for i in range(3):
        part_copy(i).wait_send()
        stat_copy(i).wait_send()
        remote(part_send.at[0], part_recv.at[i], ps_send.at[0], ps_recv.at[i], at(dz=1)).wait_recv()
        remote(stat_send.at[0], stat_recv.at[i], st_send.at[0], st_recv.at[i], at(dz=1)).wait_recv()
    peaks = [stat_send[3]] + [stat_recv[i] for i in range(3)]
    top = functools.reduce(jnp.maximum, peaks)
    factors = [jnp.exp(l - top) for l in peaks]
    inverse = 1.0 / sum(f * pltpu.roll(l, 112, 1) for f, l in zip(factors, peaks))
    real = lax.broadcasted_iota(jnp.int32, (CH, 128), 1) < 16
    total = jnp.zeros((CH, 1024), F32)
    for g in range(4):
        share = jnp.where(real, factors[g] * inverse, 0.0)
        high = share.astype(BF)
        low = (share - high.astype(F32)).astype(BF)
        wide = dot(high, expand[...]) + dot(low, expand[...])
        part = part_send[3] if g == 0 else part_recv[g - 1]
        total = total + wide * part.astype(F32)
    own_rows = pl.ds(pl.multiple_of(z * CH, CH), CH)
    pooled[own_rows, :] = total.astype(BF)

    def pool_copy(d):
        return remote(
            pooled.at[own_rows, :], pooled.at[own_rows, :],
            pool_send.at[d - 1], pool_recv.at[3 - d], at(dz=d),
        )

    for d in (1, 3, 2):
        pool_copy(d).start()

    def relayout(i, _):
        slot = lax.rem(i, 2)
        w2_copy(i, slot).wait()
        wf[...] = wstage[slot].astype(F32)
        rows = pl.ds(pl.multiple_of(i * 128, 128), 128)
        for n in range(12):
            wq[rows, n * 128 : (n + 1) * 128] = wf[pl.ds(n, 128, stride=12), :].astype(BF)

        @pl.when(i < 14)
        def _():
            w2_copy(i + 2, slot).start()

        return 0

    lax.fori_loop(0, 16, relayout, 0)
    proj_copy.wait()

    for d in (1, 2, 3):
        src_rows = pl.ds(pl.multiple_of(lax.rem(z + d, 4) * CH, CH), CH)
        remote(
            pooled.at[src_rows, :], pooled.at[src_rows, :],
            pool_send.at[0], pool_recv.at[d - 1], at(dz=d),
        ).wait_recv()

    def project(i, _):
        cs = pl.ds(pl.multiple_of(i * 512, 512), 512)
        emb[:, cs] = dot(pooled[...], proj[:, cs])
        return 0

    lax.fori_loop(0, 4, project, 0)

    def norm(i, _):
        rows = pl.ds(pl.multiple_of(i * 128, 128), 128)
        block = emb[rows, :]
        center = block - jnp.mean(block, axis=1, keepdims=True)
        variance = jnp.mean(center * center, axis=1, keepdims=True)
        normed[rows, :] = (center / jnp.sqrt(variance + 1e-05) * gain_ref[...]).astype(BF)
        return 0

    lax.fori_loop(0, 4, norm, 0)

    queries = dot(normed[...], wq[:, 0:512]) * Q_SCALE
    for h in range(4):
        q4[h] = queries[:, h * 128 : (h + 1) * 128].astype(BF)
    keys = dot(normed[...], wq[:, 512:1024])
    for h in range(4):
        kv4[h, 0:512, :] = keys[:, h * 128 : (h + 1) * 128].astype(BF)
    values = dot(normed[...], wq[:, 1024:1536])
    for h in range(4):
        for j in range(4):
            tile = values[j * 128 : (j + 1) * 128, h * 128 : (h + 1) * 128]
            kv4[h, 512 + j * 128 : 512 + (j + 1) * 128, :] = tile.T.astype(BF)

    def q_copy(d):
        dst = order((4 - d) % 4)
        head = lax.rem(x + d, 4)
        return remote(q4.at[head], q_buf.at[dst], q_send.at[d - 1], q_recv.at[dst - 1], at(dx=d))

    def kvx_copy(d):
        dst = order((4 - d) % 4)
        head = lax.rem(x + d, 4)
        return remote(kv4.at[head], kv.at[dst], kvx_send.at[d - 1], kv_recv.at[dst], at(dx=d))

    def own_copy(n, k):
        device = (at(dc=1), at(dy=1), at(dy=3), at(dy=2))[k]
        slot = n + (4, 16, 8, 24)[k]
        return remote(kv.at[n], kv.at[slot], own_send.at[n * 4 + k], kv_recv.at[slot], device)

    def fwd_copy(n):
        index = lax.div(n - 8, 8) * 4 + lax.rem(n, 4)
        return remote(
            kv.at[n], kv.at[n + 4], fwd_send.at[index], kv_recv.at[n + 4], at(dc=1)
        )

    for d in (1, 3, 2):
        q_copy(d).start()
    for d in (1, 3, 2):
        kvx_copy(d).start()
    q_buf[0] = q4[x]
    kv[0] = kv4[x]
    for k in range(3):
        own_copy(0, k).start()

    my_cols = pl.ds(pl.multiple_of(z * 512, 512), 512)
    ow_own = pltpu.make_async_copy(ow_hbm.at[:, my_cols], ow.at[z], sem_ow_own)
    ow_own.start()

    def ow_copy(d):
        cols = pl.ds(pl.multiple_of(lax.rem(z + d, 4) * 512, 512), 512)
        return remote(
            ow_hbm.at[:, cols], ow.at[z], ow_send.at[d - 1], ow_recv.at[3 - d], at(dz=d)
        )

    for d in (1, 3, 2):
        ow_copy(d).start()

    def arrive(n):
        remote(kv.at[n], kv.at[n], own_send.at[0], kv_recv.at[n], at(dc=1)).wait_recv()
        section = lax.div(n, 4)

        @pl.when(section == 0)
        def _():
            for k in range(3):
                own_copy(n, k).start()

        @pl.when(section == 1)
        def _():
            own_copy(n - 4, 3).start()

        @pl.when(jnp.logical_and(section >= 2, lax.rem(section, 2) == 0))
        def _():
            fwd_copy(n).start()

    for r in range(3):
        remote(q_buf.at[0], q_buf.at[r + 1], q_send.at[0], q_recv.at[r], at(dx=1)).wait_recv()
    acc[...] = jnp.zeros_like(acc)
    mref[...] = jnp.full_like(mref, -1e30)
    tiles = (s0, s1)
    ones = jnp.ones((16, 512), BF)

    def logits(n, t, slot):
        s = lax.dot_general(kv[n, 0:512, :], q_buf[t], NT, preferred_element_type=F32)
        tiles[slot][...] = s
        return jnp.max(s, axis=0, keepdims=True)

    def fold(n, t, slot, block_max):
        old = mref[t, 0:1, :]
        new = jnp.maximum(old, block_max)
        mref[t, 0:1, :] = new
        p = jnp.exp2(tiles[slot][...] - new).astype(BF)
        vt = jnp.concatenate([kv[n, 512 + j * 128 : 640 + j * 128, :] for j in range(4)], axis=1)
        vt = jnp.concatenate([vt, ones], axis=0)
        acc[t] = acc[t] * jnp.exp2(old - new) + dot(vt, p)

    first = logits(0, 0, 0)

    def block_step(n, block_max):
        @pl.when(n < 31)
        def _():
            arrive(n + 1)

        for u in range(4):
            ahead = n if u < 3 else jnp.minimum(n + 1, 31)
            following = logits(ahead, (u + 1) % 4, (u + 1) % 2)
            fold(n, u, u % 2, block_max)
            block_max = following
        return block_max

    lax.fori_loop(0, 32, block_step, first)

    mine = z * 4 + x

    def ax_copy(r):
        dx = order(r)
        back = order((4 - dx) % 4)
        return remote(
            stage.at[r - 1], att.at[mine], ax_send.at[r - 1], ax_recv.at[back - 1], at(dx=dx)
        )

    for r in (3, 2, 1, 0):
        a = acc[r]
        block = (a[0:128] / a[128:129]).T.astype(BF)
        if r == 0:
            att[mine] = block
        else:
            stage[r - 1] = block
            ax_copy(r).start()

    def az_copy(r, d):
        head = z * 4 + lax.rem(x + order(r), 4)
        return remote(
            att.at[head], att.at[head], az_send.at[r * 3 + d - 1], az_recv.at[r * 3 + 3 - d],
            at(dz=d),
        )

    for r in (0, 3, 1, 2):
        if r > 0:
            head = z * 4 + lax.rem(x + order(r), 4)
            remote(
                stage.at[0], att.at[head], ax_send.at[0], ax_recv.at[r - 1], at(dx=1)
            ).wait_recv()
        for d in (1, 3, 2):
            az_copy(r, d).start()

    ow_own.wait()
    for d in (1, 2, 3):
        src = lax.rem(z + d, 4)
        remote(
            ow.at[src], ow.at[src], ow_send.at[0], ow_recv.at[d - 1], at(dz=1)
        ).wait_recv()
    for r in range(4):
        for d in (1, 2, 3):
            head = lax.rem(z + d, 4) * 4 + lax.rem(x + order(r), 4)
            remote(
                att.at[head], att.at[head], az_send.at[0], az_recv.at[r * 3 + d - 1], at(dz=1)
            ).wait_recv()

    result = emb[:, my_cols]
    for g in range(4):
        heads = jnp.concatenate([att[g * 4 + h] for h in range(4)], axis=1)
        result = result + dot(heads, ow[g])
    out_ref[...] = result.astype(BF)

    for d in (1, 2, 3):
        pool_copy(d).wait_send()
        q_copy(d).wait_send()
        kvx_copy(d).wait_send()
        ow_copy(d).wait_send()
        ax_copy(d).wait_send()
        for r in range(4):
            az_copy(r, d).wait_send()

    def drain(n, _):
        for k in range(4):
            own_copy(n, k).wait_send()
        return 0

    lax.fori_loop(0, 4, drain, 0)

    def drain_fwd(i, _):
        fwd_copy(8 + lax.div(i, 4) * 8 + lax.rem(i, 4)).wait_send()
        return 0

    lax.fori_loop(0, 12, drain_fwd, 0)


def on_device(tokens, key_query, value_weight, proj_weight, norm_gain, qkv_weight, out_weight):
    dma = pltpu.SemaphoreType.DMA
    vm = pltpu.VMEM
    scratch = [
        vm((2, NV, CH, 1024), BF),
        vm((128, 1024), BF),
        vm((128, 1024), BF),
        vm((1024, 1024), BF),
        vm((1024, 2048), BF),
        vm((2, 1536, 128), BF),
        vm((1536, 128), F32),
        vm((2048, 1536), BF),
        vm((NV * CH, 128), BF),
        vm((4, CH, 1024), BF),
        vm((3, CH, 1024), BF),
        vm((4, CH, 128), F32),
        vm((3, CH, 128), F32),
        vm((ROWS, 1024), BF),
        vm((ROWS, 2048), F32),
        vm((ROWS, 2048), BF),
        vm((4, ROWS, 128), BF),
        vm((4, 2 * ROWS, 128), BF),
        vm((4, ROWS, 128), BF),
        vm((32, 2 * ROWS, 128), BF),
        vm((512, 512), F32),
        vm((512, 512), F32),
        vm((4, 144, 512), F32),
        vm((4, 8, 512), F32),
        vm((4, 512, 512), BF),
        vm((3, ROWS, 128), BF),
        vm((16, ROWS, 128), BF),
        dma((2,)), dma((2,)), dma((2,)), dma,
        dma((3,)), dma((3,)), dma((3,)), dma((3,)), dma((3,)), dma((3,)),
        dma((3,)), dma((3,)), dma((3,)), dma((16,)), dma((12,)), dma((32,)),
        dma((3,)), dma((3,)), dma((3,)), dma((3,)), dma((12,)), dma((12,)),
    ]
    anywhere = pl.BlockSpec(memory_space=pl.ANY)
    vmem = pl.BlockSpec(memory_space=pltpu.VMEM)
    return pl.pallas_call(
        kernel,
        out_shape=jax.ShapeDtypeStruct((ROWS, 512), BF),
        in_specs=[anywhere, vmem, anywhere, anywhere, vmem, anywhere, anywhere],
        out_specs=vmem,
        scratch_shapes=scratch,
        compiler_params=pltpu.CompilerParams(
            collective_id=1, has_side_effects=True, vmem_limit_bytes=62 * 1024 * 1024
        ),
        name="block",
    )(
        tokens,
        key_query.T,
        value_weight,
        proj_weight,
        norm_gain.reshape(1, 2048),
        qkv_weight.reshape(2048 * 12, 128),
        out_weight.reshape(512, 2048),
    )


def solution(mesh):
    return jax.shard_map(
        on_device,
        mesh=mesh,
        in_specs=(
            P("var", "patch", None),
            P(),
            P(),
            P(),
            P(),
            P(None, None, "var", None),
            P("var", None, None),
        ),
        out_specs=P("patch", "var"),
        check_vma=False,
    )
```

time: 594 us -> 154 us (0.26)
  the two profiles are of different devices: /device:TPU:0 before, /device:TPU:16 now
where the time goes in v1:
time: 154 us; the launch traced here: 153 us
  Pallas kernels  152 us (99%)
  local copies, waits for them, and re-layouts  1.87 us (1%)
    pallas_call x1, Pallas kernels, on_device(): pl.pallas_call(kernel, out_shape=jax.ShapeDtypeStruct((ROWS, 512), BF), i...  152 us

profile of v1, /device:TPU:16, one launch (start us, length us, event | category | flops | bytes accessed | tf_op | source)
XLA Modules:
  0.0 153.4 jit_solution(9402861209549926924)
XLA Ops:
  0.0 151.5 %block.1 = bf16[512,512]{1,0:T(8,128)(2,1)} custom-call(bf16[12,512,1024]{2,1,0:T(8,128)(2,1)} %tok_hbm.1, bf16[16,1024]{1,0:T(8,128)(2,1)} %bitcast.6, bf16[1024,1024]{1,0:T(8,128)(2,1)} %vw_hbm.1, bf16[1024,2048]{1,0:T(8,128)(2,1)} %proj_hbm.1, f32[1,2048]{1,0:T(1,128)} %bitcast.7, bf16[24576,128]{1,0:T(8,128)(2,1)} %bitcast.4, bf16[512,2048]{1,0:T(8,128)(2,1)} %bitcast.5), custom_call_target="tpu_custom_call" | custom-call | tf_op jit(solution)/shard_map/block/pallas_call | solution.py:438
  151.5 1.9 %copy.9 = bf16[512,512]{1,0:T(8,128)(2,1)} copy(bf16[512,512]{1,0:T(8,128)(2,1)} %block.1) | data formatting | bytes 1048576

commit v2 on v1

--- a/solution.py
+++ b/solution.py
@@ -13,6 +13,7 @@
 F32 = jnp.float32
 
 ROWS, NV, CH = 512, 12, 128
+EARLY = 24
 Q_SCALE = 128 ** (-0.5) * 1.4426950408889634
 
 
@@ -83,7 +84,6 @@
     partners += [at(dz=d) for d in (1, 2, 3)] + [at(dc=1)]
     for device in partners:
         pl.semaphore_signal(barrier, inc=1, device_id=device, device_id_type=MESH)
-    pl.semaphore_wait(barrier, len(partners))
 
     kqp[...] = jnp.zeros_like(kqp)
     kqp[0:16, :] = kq_ref[...]
@@ -131,6 +131,10 @@
         @pl.when(j < 2)
         def _():
             tok_copy(j + 2, slot).start()
+
+        @pl.when(j == 0)
+        def _():
+            pl.semaphore_wait(barrier, len(partners))
 
         @pl.when(j < 3)
         def _():
@@ -177,7 +181,8 @@
         wf[...] = wstage[slot].astype(F32)
         rows = pl.ds(pl.multiple_of(i * 128, 128), 128)
         for n in range(12):
-            wq[rows, n * 128 : (n + 1) * 128] = wf[pl.ds(n, 128, stride=12), :].astype(BF)
+            to = n if n < 4 else 4 + 2 * (n % 4) + n // 8
+            wq[rows, to * 128 : (to + 1) * 128] = wf[pl.ds(n, 128, stride=12), :].astype(BF)
 
         @pl.when(i < 14)
         def _():
@@ -212,22 +217,12 @@
 
     lax.fori_loop(0, 4, norm, 0)
 
-    queries = dot(normed[...], wq[:, 0:512]) * Q_SCALE
-    for h in range(4):
-        q4[h] = queries[:, h * 128 : (h + 1) * 128].astype(BF)
-    keys = dot(normed[...], wq[:, 512:1024])
-    for h in range(4):
-        kv4[h, 0:512, :] = keys[:, h * 128 : (h + 1) * 128].astype(BF)
-    values = dot(normed[...], wq[:, 1024:1536])
-    for h in range(4):
-        for j in range(4):
-            tile = values[j * 128 : (j + 1) * 128, h * 128 : (h + 1) * 128]
-            kv4[h, 512 + j * 128 : 512 + (j + 1) * 128, :] = tile.T.astype(BF)
-
     def q_copy(d):
         dst = order((4 - d) % 4)
         head = lax.rem(x + d, 4)
-        return remote(q4.at[head], q_buf.at[dst], q_send.at[d - 1], q_recv.at[dst - 1], at(dx=d))
+        return remote(
+            q4.at[head], q_buf.at[3 - dst], q_send.at[d - 1], q_recv.at[dst - 1], at(dx=d)
+        )
 
     def kvx_copy(d):
         dst = order((4 - d) % 4)
@@ -245,14 +240,35 @@
             kv.at[n], kv.at[n + 4], fwd_send.at[index], kv_recv.at[n + 4], at(dc=1)
         )
 
-    for d in (1, 3, 2):
+    queries = dot(normed[...], wq[:, 0:512]) * Q_SCALE
+    for h in range(4):
+        q4[h] = queries[:, h * 128 : (h + 1) * 128].astype(BF)
+    for d in (2, 1, 3):
         q_copy(d).start()
-    for d in (1, 3, 2):
-        kvx_copy(d).start()
-    q_buf[0] = q4[x]
-    kv[0] = kv4[x]
+    q_buf[3] = q4[x]
+
+    def keys_values(head, write):
+        cs = pl.ds(pl.multiple_of(512 + head * 256, 256), 256)
+        both = dot(normed[...], wq[:, cs])
+        write(slice(0, 512), both[:, 0:128].astype(BF))
+        for j in range(4):
+            tile = both[j * 128 : (j + 1) * 128, 128:256]
+            write(slice(512 + j * 128, 640 + j * 128), tile.T.astype(BF))
+
+    def write_own(rows, value):
+        kv[0, rows, :] = value
+
+    keys_values(x, write_own)
     for k in range(3):
         own_copy(0, k).start()
+    for d in (1, 3, 2):
+        head = lax.rem(x + d, 4)
+
+        def write_other(rows, value, head=head):
+            kv4[head, rows, :] = value
+
+        keys_values(head, write_other)
+        kvx_copy(d).start()
 
     my_cols = pl.ds(pl.multiple_of(z * 512, 512), 512)
     ow_own = pltpu.make_async_copy(ow_hbm.at[:, my_cols], ow.at[z], sem_ow_own)
@@ -285,7 +301,7 @@
             fwd_copy(n).start()
 
     for r in range(3):
-        remote(q_buf.at[0], q_buf.at[r + 1], q_send.at[0], q_recv.at[r], at(dx=1)).wait_recv()
+        remote(q_buf.at[3], q_buf.at[2 - r], q_send.at[0], q_recv.at[r], at(dx=1)).wait_recv()
     acc[...] = jnp.zeros_like(acc)
     mref[...] = jnp.full_like(mref, -1e30)
     tiles = (s0, s1)
@@ -308,52 +324,81 @@
     first = logits(0, 0, 0)
 
     def block_step(n, block_max):
-        @pl.when(n < 31)
-        def _():
-            arrive(n + 1)
-
+        arrive(n + 1)
         for u in range(4):
-            ahead = n if u < 3 else jnp.minimum(n + 1, 31)
+            ahead = n if u < 3 else n + 1
             following = logits(ahead, (u + 1) % 4, (u + 1) % 2)
             fold(n, u, u % 2, block_max)
             block_max = following
         return block_max
 
-    lax.fori_loop(0, 32, block_step, first)
+    carry = lax.fori_loop(0, EARLY, block_step, first)
+    for n in range(EARLY + 1, 32):
+        arrive(n)
 
     mine = z * 4 + x
 
-    def ax_copy(r):
-        dx = order(r)
-        back = order((4 - dx) % 4)
-        return remote(
-            stage.at[r - 1], att.at[mine], ax_send.at[r - 1], ax_recv.at[back - 1], at(dx=dx)
-        )
-
-    for r in (3, 2, 1, 0):
-        a = acc[r]
+    def ax_copy(t):
+        dx = order(3 - t)
+        back = order((4 - dx) % 4) if isinstance(dx, int) else order(lax.rem(4 - dx, 4))
+        return remote(
+            stage.at[t], att.at[mine], ax_send.at[t], ax_recv.at[3 - back], at(dx=dx)
+        )
+
+    def az_copy(t, d):
+        head = z * 4 + lax.rem(x + order(3 - t), 4)
+        return remote(
+            att.at[head], att.at[head], az_send.at[t * 3 + d - 1], az_recv.at[t * 3 + 3 - d],
+            at(dz=d),
+        )
+
+    def share(t):
+        for d in (2, 1, 3):
+            az_copy(t, d).start()
+
+    def ax_arrive(t):
+        head = z * 4 + lax.rem(x + order(3 - t), 4)
+        remote(stage.at[0], att.at[head], ax_send.at[0], ax_recv.at[t], at(dx=1)).wait_recv()
+
+    def tile_step(t, block_max):
+        def group(i, block_max):
+            base = EARLY + i * 4
+            last = i == (32 - EARLY) // 4 - 1
+            for u in range(4):
+                if u < 3:
+                    following = logits(base + u + 1, t, (u + 1) % 2)
+                else:
+                    following = logits(
+                        jnp.where(last, EARLY, base + 4),
+                        jnp.where(last, jnp.minimum(t + 1, 3), t),
+                        0,
+                    )
+                fold(base + u, t, u % 2, block_max)
+                block_max = following
+            return block_max
+
+        block_max = lax.fori_loop(0, (32 - EARLY) // 4, group, block_max)
+        a = acc[t]
         block = (a[0:128] / a[128:129]).T.astype(BF)
-        if r == 0:
+
+        @pl.when(t < 3)
+        def _():
+            stage[t] = block
+            ax_copy(t).start()
+
+        @pl.when(t == 3)
+        def _():
             att[mine] = block
-        else:
-            stage[r - 1] = block
-            ax_copy(r).start()
-
-    def az_copy(r, d):
-        head = z * 4 + lax.rem(x + order(r), 4)
-        return remote(
-            att.at[head], att.at[head], az_send.at[r * 3 + d - 1], az_recv.at[r * 3 + 3 - d],
-            at(dz=d),
-        )
-
-    for r in (0, 3, 1, 2):
-        if r > 0:
-            head = z * 4 + lax.rem(x + order(r), 4)
-            remote(
-                stage.at[0], att.at[head], ax_send.at[0], ax_recv.at[r - 1], at(dx=1)
-            ).wait_recv()
-        for d in (1, 3, 2):
-            az_copy(r, d).start()
+            share(3)
+
+        @pl.when(t > 0)
+        def _():
+            ax_arrive(t - 1)
+            share(t - 1)
+
+        return block_max
+
+    lax.fori_loop(0, 4, tile_step, carry)
 
     ow_own.wait()
     for d in (1, 2, 3):
@@ -361,11 +406,11 @@
         remote(
             ow.at[src], ow.at[src], ow_send.at[0], ow_recv.at[d - 1], at(dz=1)
         ).wait_recv()
-    for r in range(4):
+    for t in range(4):
         for d in (1, 2, 3):
-            head = lax.rem(z + d, 4) * 4 + lax.rem(x + order(r), 4)
+            head = lax.rem(z + d, 4) * 4 + lax.rem(x + order(3 - t), 4)
             remote(
-                att.at[head], att.at[head], az_send.at[0], az_recv.at[r * 3 + d - 1], at(dz=1)
+                att.at[head], att.at[head], az_send.at[0], az_recv.at[t * 3 + d - 1], at(dz=1)
             ).wait_recv()
 
     result = emb[:, my_cols]
@@ -379,9 +424,9 @@
         q_copy(d).wait_send()
         kvx_copy(d).wait_send()
         ow_copy(d).wait_send()
-        ax_copy(d).wait_send()
-        for r in range(4):
-            az_copy(r, d).wait_send()
+        ax_copy(d - 1).wait_send()
+        for t in range(4):
+            az_copy(t, d).wait_send()
 
     def drain(n, _):
         for k in range(4):

time: 154 us -> 151 us (0.981)
  the two profiles are of different devices: /device:TPU:16 before, /device:TPU:0 now
where the time goes in v2:
time: 151 us; the launch traced here: 149 us
  Pallas kernels  147 us (97%)
  local copies, waits for them, and re-layouts  1.87 us (1%)
    pallas_call x1, Pallas kernels, on_device(): pl.pallas_call(kernel, out_shape=jax.ShapeDtypeStruct((ROWS, 512), BF), i...  147 us

profile of v2, /device:TPU:0, one launch (start us, length us, event | category | flops | bytes accessed | tf_op | source)
XLA Modules:
  0.0 149.0 jit_solution(473897686128383084)
XLA Ops:
  0.0 147.1 %block.1 = bf16[512,512]{1,0:T(8,128)(2,1)} custom-call(bf16[12,512,1024]{2,1,0:T(8,128)(2,1)} %tok_hbm.1, bf16[16,1024]{1,0:T(8,128)(2,1)} %bitcast.6, bf16[1024,1024]{1,0:T(8,128)(2,1)} %vw_hbm.1, bf16[1024,2048]{1,0:T(8,128)(2,1)} %proj_hbm.1, f32[1,2048]{1,0:T(1,128)} %bitcast.7, bf16[24576,128]{1,0:T(8,128)(2,1)} %bitcast.4, bf16[512,2048]{1,0:T(8,128)(2,1)} %bitcast.5), custom_call_target="tpu_custom_call" | custom-call | tf_op jit(solution)/shard_map/block/pallas_call | solution.py:483
  147.1 1.9 %copy.9 = bf16[512,512]{1,0:T(8,128)(2,1)} copy(bf16[512,512]{1,0:T(8,128)(2,1)} %block.1) | data formatting | bytes 1048576

commit v3 on v2

--- a/solution.py
+++ b/solution.py
@@ -13,7 +13,7 @@
 F32 = jnp.float32
 
 ROWS, NV, CH = 512, 12, 128
-EARLY = 24
+EARLY = 20
 Q_SCALE = 128 ** (-0.5) * 1.4426950408889634
 
 
@@ -36,7 +36,7 @@
     ow, stage, att,
     sem_tok, sem_w, sem_w2, sem_ow_own,
     ps_send, ps_recv, st_send, st_recv, pool_send, pool_recv,
-    q_send, q_recv, kvx_send, own_send, fwd_send, kv_recv,
+    q_send, q_recv, kvx_send, own_send, fwd_send, hop_send, kv_recv,
     ow_send, ow_recv, ax_send, ax_recv, az_send, az_recv,
 ):
     z = lax.axis_index("var")
@@ -104,6 +104,19 @@
         return remote(
             stat_send.at[j], stat_recv.at[3 - dz], st_send.at[j], st_recv.at[3 - dz], at(dz=dz)
         )
+
+    def relayout(i):
+        slot = lax.rem(i, 2)
+        w2_copy(i, slot).wait()
+        wf[...] = wstage[slot].astype(F32)
+        rows = pl.ds(pl.multiple_of(i * 128, 128), 128)
+        for n in range(12):
+            to = n if n < 4 else 4 + 2 * (n % 4) + n // 8
+            wq[rows, to * 128 : (to + 1) * 128] = wf[pl.ds(n, 128, stride=12), :].astype(BF)
+
+        @pl.when(i < 14)
+        def _():
+            w2_copy(i + 2, slot).start()
 
     def pool_chunk(j, _):
         slot = lax.rem(j, 2)
@@ -124,6 +137,7 @@
             wide = dot(wn[...], expand[:, cs])
             summed = jnp.sum((values * wide).reshape(NV, CH, 256), axis=0)
             part_send[j, :, cs] = summed.astype(BF)
+            relayout(j * 4 + i)
             return 0
 
         lax.fori_loop(0, 4, columns, 0)
@@ -166,39 +180,28 @@
     own_rows = pl.ds(pl.multiple_of(z * CH, CH), CH)
     pooled[own_rows, :] = total.astype(BF)
 
-    def pool_copy(d):
-        return remote(
-            pooled.at[own_rows, :], pooled.at[own_rows, :],
-            pool_send.at[d - 1], pool_recv.at[3 - d], at(dz=d),
-        )
-
-    for d in (1, 3, 2):
-        pool_copy(d).start()
-
-    def relayout(i, _):
-        slot = lax.rem(i, 2)
-        w2_copy(i, slot).wait()
-        wf[...] = wstage[slot].astype(F32)
-        rows = pl.ds(pl.multiple_of(i * 128, 128), 128)
-        for n in range(12):
-            to = n if n < 4 else 4 + 2 * (n % 4) + n // 8
-            wq[rows, to * 128 : (to + 1) * 128] = wf[pl.ds(n, 128, stride=12), :].astype(BF)
-
-        @pl.when(i < 14)
-        def _():
-            w2_copy(i + 2, slot).start()
-
-        return 0
-
-    lax.fori_loop(0, 16, relayout, 0)
+    def pool_rows(dz, half=None):
+        base = lax.rem(z + dz, 4) * CH
+        if half is None:
+            return pooled.at[pl.ds(pl.multiple_of(base, CH), CH), :]
+        return pooled.at[pl.ds(pl.multiple_of(base + half * (CH // 2), CH // 2), CH // 2), :]
+
+    def pool_copy(i):
+        rows = (pool_rows(0), pool_rows(0), pool_rows(3, 0), pool_rows(1, 1))[i]
+        return remote(rows, rows, pool_send.at[i], pool_recv.at[i], at(dz=(1, 3, 1, 3)[i]))
+
+    def pool_arrive(i):
+        rows = (pool_rows(3), pool_rows(1), pool_rows(2, 0), pool_rows(2, 1))[i]
+        remote(rows, rows, pool_send.at[0], pool_recv.at[i], at(dz=1)).wait_recv()
+
+    pool_copy(0).start()
+    pool_copy(1).start()
     proj_copy.wait()
-
-    for d in (1, 2, 3):
-        src_rows = pl.ds(pl.multiple_of(lax.rem(z + d, 4) * CH, CH), CH)
-        remote(
-            pooled.at[src_rows, :], pooled.at[src_rows, :],
-            pool_send.at[0], pool_recv.at[d - 1], at(dz=d),
-        ).wait_recv()
+    for i in (0, 1):
+        pool_arrive(i)
+        pool_copy(i + 2).start()
+    for i in (2, 3):
+        pool_arrive(i)
 
     def project(i, _):
         cs = pl.ds(pl.multiple_of(i * 512, 512), 512)
@@ -230,14 +233,22 @@
         return remote(kv4.at[head], kv.at[dst], kvx_send.at[d - 1], kv_recv.at[dst], at(dx=d))
 
     def own_copy(n, k):
-        device = (at(dc=1), at(dy=1), at(dy=3), at(dy=2))[k]
-        slot = n + (4, 16, 8, 24)[k]
-        return remote(kv.at[n], kv.at[slot], own_send.at[n * 4 + k], kv_recv.at[slot], device)
+        device = (at(dc=1), at(dy=1), at(dy=3))[k]
+        slot = (n + 4, 9 + 2 * n, 8 + 2 * n)[k]
+        return remote(kv.at[n], kv.at[slot], own_send.at[n * 3 + k], kv_recv.at[slot], device)
 
     def fwd_copy(n):
-        index = lax.div(n - 8, 8) * 4 + lax.rem(n, 4)
-        return remote(
-            kv.at[n], kv.at[n + 4], fwd_send.at[index], kv_recv.at[n + 4], at(dc=1)
+        late = lax.div(n, 24)
+        return remote(
+            kv.at[n], kv.at[n + 8 - 4 * late], fwd_send.at[n - 8 - 8 * late],
+            kv_recv.at[n + 8 - 4 * late], at(dc=1),
+        )
+
+    def hop_copy(n):
+        r = lax.div(n - 8, 2)
+        up = lax.rem(n, 2)
+        return remote(
+            kv.at[n], kv.at[24 + r], hop_send.at[r], kv_recv.at[24 + r], at(dy=3 - 2 * up)
         )
 
     queries = dot(normed[...], wq[:, 0:512]) * Q_SCALE
@@ -285,18 +296,19 @@
 
     def arrive(n):
         remote(kv.at[n], kv.at[n], own_send.at[0], kv_recv.at[n], at(dc=1)).wait_recv()
-        section = lax.div(n, 4)
-
-        @pl.when(section == 0)
+
+        @pl.when(n < 4)
         def _():
             for k in range(3):
                 own_copy(n, k).start()
 
-        @pl.when(section == 1)
-        def _():
-            own_copy(n - 4, 3).start()
-
-        @pl.when(jnp.logical_and(section >= 2, lax.rem(section, 2) == 0))
+        near = jnp.logical_and(n >= 8, n < 16)
+
+        @pl.when(jnp.logical_and(near, lax.rem(n, 2) == jnp.where(n < 12, 1, 0)))
+        def _():
+            hop_copy(n).start()
+
+        @pl.when(jnp.logical_or(near, jnp.logical_and(n >= 24, n < 28)))
         def _():
             fwd_copy(n).start()
 
@@ -333,8 +345,12 @@
         return block_max
 
     carry = lax.fori_loop(0, EARLY, block_step, first)
-    for n in range(EARLY + 1, 32):
+
+    def arrive_late(n, _):
         arrive(n)
+        return 0
+
+    lax.fori_loop(EARLY + 1, 32, arrive_late, 0)
 
     mine = z * 4 + x
 
@@ -345,16 +361,30 @@
             stage.at[t], att.at[mine], ax_send.at[t], ax_recv.at[3 - back], at(dx=dx)
         )
 
-    def az_copy(t, d):
-        head = z * 4 + lax.rem(x + order(3 - t), 4)
-        return remote(
-            att.at[head], att.at[head], az_send.at[t * 3 + d - 1], az_recv.at[t * 3 + 3 - d],
-            at(dz=d),
-        )
+    def az_rows(t, dz, half=None):
+        head = lax.rem(z + dz, 4) * 4 + lax.rem(x + order(3 - t), 4)
+        if half is None:
+            return att.at[head]
+        return att.at[head, pl.ds(half * 256, 256), :]
+
+    def az_copy(t, i):
+        rows = (az_rows(t, 0), az_rows(t, 0), az_rows(t, 3, 0), az_rows(t, 1, 1))[i]
+        return remote(
+            rows, rows, az_send.at[t * 4 + i], az_recv.at[t * 4 + i], at(dz=(1, 3, 1, 3)[i])
+        )
+
+    def az_arrive(t, i):
+        rows = (az_rows(t, 3), az_rows(t, 1), az_rows(t, 2, 0), az_rows(t, 2, 1))[i]
+        remote(rows, rows, az_send.at[0], az_recv.at[t * 4 + i], at(dz=1)).wait_recv()
 
     def share(t):
-        for d in (2, 1, 3):
-            az_copy(t, d).start()
+        az_copy(t, 0).start()
+        az_copy(t, 1).start()
+
+    def relay(t):
+        for i in (0, 1):
+            az_arrive(t, i)
+            az_copy(t, i + 2).start()
 
     def ax_arrive(t):
         head = z * 4 + lax.rem(x + order(3 - t), 4)
@@ -396,47 +426,55 @@
             ax_arrive(t - 1)
             share(t - 1)
 
+        @pl.when(t > 1)
+        def _():
+            relay(t - 2)
+
         return block_max
 
     lax.fori_loop(0, 4, tile_step, carry)
+
+    def branch(dz):
+        zs = lax.rem(z + dz, 4)
+        heads = jnp.concatenate([att[zs * 4 + h] for h in range(4)], axis=1)
+        return dot(heads, ow[zs])
+
+    def ow_arrive(d):
+        src = lax.rem(z + d, 4)
+        remote(ow.at[src], ow.at[src], ow_send.at[0], ow_recv.at[d - 1], at(dz=1)).wait_recv()
 
     ow_own.wait()
     for d in (1, 2, 3):
-        src = lax.rem(z + d, 4)
-        remote(
-            ow.at[src], ow.at[src], ow_send.at[0], ow_recv.at[d - 1], at(dz=1)
-        ).wait_recv()
+        ow_arrive(d)
+    result = emb[:, my_cols] + branch(0)
+    relay(2)
+    relay(3)
+    result = result + branch(1) + branch(3)
     for t in range(4):
-        for d in (1, 2, 3):
-            head = lax.rem(z + d, 4) * 4 + lax.rem(x + order(3 - t), 4)
-            remote(
-                att.at[head], att.at[head], az_send.at[0], az_recv.at[t * 3 + d - 1], at(dz=1)
-            ).wait_recv()
-
-    result = emb[:, my_cols]
-    for g in range(4):
-        heads = jnp.concatenate([att[g * 4 + h] for h in range(4)], axis=1)
-        result = result + dot(heads, ow[g])
-    out_ref[...] = result.astype(BF)
-
+        az_arrive(t, 2)
+        az_arrive(t, 3)
+    out_ref[...] = (result + branch(2)).astype(BF)
+
+    for i in range(4):
+        pool_copy(i).wait_send()
     for d in (1, 2, 3):
-        pool_copy(d).wait_send()
         q_copy(d).wait_send()
         kvx_copy(d).wait_send()
         ow_copy(d).wait_send()
         ax_copy(d - 1).wait_send()
-        for t in range(4):
-            az_copy(t, d).wait_send()
 
     def drain(n, _):
-        for k in range(4):
+        for k in range(3):
             own_copy(n, k).wait_send()
+        for i in range(4):
+            az_copy(n, i).wait_send()
+        hop_copy(9 + 2 * n - lax.div(n, 2)).wait_send()
         return 0
 
     lax.fori_loop(0, 4, drain, 0)
 
     def drain_fwd(i, _):
-        fwd_copy(8 + lax.div(i, 4) * 8 + lax.rem(i, 4)).wait_send()
+        fwd_copy(8 + i + 8 * lax.div(i, 8)).wait_send()
         return 0
 
     lax.fori_loop(0, 12, drain_fwd, 0)
@@ -474,9 +512,9 @@
         vm((3, ROWS, 128), BF),
         vm((16, ROWS, 128), BF),
         dma((2,)), dma((2,)), dma((2,)), dma,
-        dma((3,)), dma((3,)), dma((3,)), dma((3,)), dma((3,)), dma((3,)),
-        dma((3,)), dma((3,)), dma((3,)), dma((16,)), dma((12,)), dma((32,)),
-        dma((3,)), dma((3,)), dma((3,)), dma((3,)), dma((12,)), dma((12,)),
+        dma((3,)), dma((3,)), dma((3,)), dma((3,)), dma((4,)), dma((4,)),
+        dma((3,)), dma((3,)), dma((3,)), dma((12,)), dma((12,)), dma((4,)), dma((32,)),
+        dma((3,)), dma((3,)), dma((3,)), dma((3,)), dma((16,)), dma((16,)),
     ]
     anywhere = pl.BlockSpec(memory_space=pl.ANY)
     vmem = pl.BlockSpec(memory_space=pltpu.VMEM)

time: 151 us -> 135 us (0.89); the launches traced: 149 us -> 135 us
  Pallas kernels: 147 us -> 133 us
    pallas_call x1, Pallas kernels: 147 us -> 133 us  [on_device(): pl.pallas_call(kernel, out_shape=jax.ShapeDtypeStruct((ROWS, 512), BF), i...]
where the time goes in v3:
time: 135 us
  Pallas kernels  133 us (99%)
  local copies, waits for them, and re-layouts  1.87 us (1%)
    pallas_call x1, Pallas kernels, on_device(): pl.pallas_call(kernel, out_shape=jax.ShapeDtypeStruct((ROWS, 512), BF), i...  133 us

profile of v3, /device:TPU:0, one launch (start us, length us, event | category | flops | bytes accessed | tf_op | source)
XLA Modules:
  0.0 134.5 jit_solution(12941266640986287282)
XLA Ops:
  0.0 132.7 %block.1 = bf16[512,512]{1,0:T(8,128)(2,1)} custom-call(bf16[12,512,1024]{2,1,0:T(8,128)(2,1)} %tok_hbm.1, bf16[16,1024]{1,0:T(8,128)(2,1)} %bitcast.6, bf16[1024,1024]{1,0:T(8,128)(2,1)} %vw_hbm.1, bf16[1024,2048]{1,0:T(8,128)(2,1)} %proj_hbm.1, f32[1,2048]{1,0:T(1,128)} %bitcast.7, bf16[24576,128]{1,0:T(8,128)(2,1)} %bitcast.4, bf16[512,2048]{1,0:T(8,128)(2,1)} %bitcast.5), custom_call_target="tpu_custom_call" | custom-call | tf_op jit(solution)/shard_map/block/pallas_call | solution.py:521
  132.7 1.9 %copy.9 = bf16[512,512]{1,0:T(8,128)(2,1)} copy(bf16[512,512]{1,0:T(8,128)(2,1)} %block.1) | data formatting | bytes 1048576

commit v4 on v3

--- a/solution.py
+++ b/solution.py
@@ -13,7 +13,7 @@
 F32 = jnp.float32
 
 ROWS, NV, CH = 512, 12, 128
-EARLY = 20
+EARLY = 12
 Q_SCALE = 128 ** (-0.5) * 1.4426950408889634
 
 
@@ -32,7 +32,7 @@
     out_ref,
     tok, kqp, expand, vw, proj, wstage, wf, wq,
     wn, part_send, part_recv, stat_send, stat_recv, pooled,
-    emb, normed, q4, kv4, q_buf, kv, s0, s1, acc, mref,
+    emb, normed, q4, kv4, q_buf, kv, s0, s1, p0, p1, acc, mref,
     ow, stage, att,
     sem_tok, sem_w, sem_w2, sem_ow_own,
     ps_send, ps_recv, st_send, st_recv, pool_send, pool_recv,
@@ -105,19 +105,6 @@
             stat_send.at[j], stat_recv.at[3 - dz], st_send.at[j], st_recv.at[3 - dz], at(dz=dz)
         )
 
-    def relayout(i):
-        slot = lax.rem(i, 2)
-        w2_copy(i, slot).wait()
-        wf[...] = wstage[slot].astype(F32)
-        rows = pl.ds(pl.multiple_of(i * 128, 128), 128)
-        for n in range(12):
-            to = n if n < 4 else 4 + 2 * (n % 4) + n // 8
-            wq[rows, to * 128 : (to + 1) * 128] = wf[pl.ds(n, 128, stride=12), :].astype(BF)
-
-        @pl.when(i < 14)
-        def _():
-            w2_copy(i + 2, slot).start()
-
     def pool_chunk(j, _):
         slot = lax.rem(j, 2)
         tok_copy(j, slot).wait()
@@ -129,18 +116,14 @@
         totals = jnp.sum(weights, axis=0)
         first_lanes = lax.broadcasted_iota(jnp.int32, (CH, 128), 1) < 16
         stat_send[j] = jnp.where(first_lanes, peak, pltpu.roll(totals, 16, 1))
-        wn[...] = weights.astype(BF).reshape(NV * CH, 128)
-
-        def columns(i, _):
-            cs = pl.ds(pl.multiple_of(i * 256, 256), 256)
-            values = dot(tok[slot].reshape(NV * CH, 1024), vw[:, cs])
-            wide = dot(wn[...], expand[:, cs])
-            summed = jnp.sum((values * wide).reshape(NV, CH, 256), axis=0)
-            part_send[j, :, cs] = summed.astype(BF)
-            relayout(j * 4 + i)
-            return 0
-
-        lax.fori_loop(0, 4, columns, 0)
+        wn[...] = weights.astype(BF).astype(F32).reshape(NV * CH, 128)
+
+        upper = jnp.where(lax.broadcasted_iota(jnp.int32, (NV * CH, 128), 1) >= 64, 1, 0)
+        values = dot(tok[slot].reshape(NV * CH, 1024), vw[...])
+        wide = jnp.concatenate(
+            [jnp.take_along_axis(wn[...], 2 * q + upper, axis=1) for q in range(8)], axis=1
+        )
+        part_send[j] = jnp.sum((values * wide).reshape(NV, CH, 1024), axis=0).astype(BF)
 
         @pl.when(j < 2)
         def _():
@@ -196,10 +179,28 @@
 
     pool_copy(0).start()
     pool_copy(1).start()
-    proj_copy.wait()
+
+    def relayout(i, _):
+        slot = lax.rem(i, 2)
+        w2_copy(i, slot).wait()
+        wf[...] = wstage[slot].astype(F32)
+        rows = pl.ds(pl.multiple_of(i * 128, 128), 128)
+        for n in range(12):
+            to = n if n < 4 else 4 + 2 * (n % 4) + n // 8
+            wq[rows, to * 128 : (to + 1) * 128] = wf[pl.ds(n, 128, stride=12), :].astype(BF)
+
+        @pl.when(i < 14)
+        def _():
+            w2_copy(i + 2, slot).start()
+
+        return 0
+
+    lax.fori_loop(0, 11, relayout, 0)
     for i in (0, 1):
         pool_arrive(i)
         pool_copy(i + 2).start()
+    lax.fori_loop(11, 16, relayout, 0)
+    proj_copy.wait()
     for i in (2, 3):
         pool_arrive(i)
 
@@ -230,25 +231,38 @@
     def kvx_copy(d):
         dst = order((4 - d) % 4)
         head = lax.rem(x + d, 4)
-        return remote(kv4.at[head], kv.at[dst], kvx_send.at[d - 1], kv_recv.at[dst], at(dx=d))
-
-    def own_copy(n, k):
+        slot = own_slot(dst)
+        return remote(kv4.at[head], kv.at[slot], kvx_send.at[d - 1], kv_recv.at[slot], at(dx=d))
+
+    def own_slot(r):
+        return (0, 6, 8, 10)[r] if isinstance(r, int) else jnp.where(r == 0, 0, 4 + 2 * r)
+
+    def near_slot(r):
+        return (2, 12, 16, 20)[r] if isinstance(r, int) else jnp.where(r == 0, 2, 8 + 4 * r)
+
+    def own_copy(r, k):
         device = (at(dc=1), at(dy=1), at(dy=3))[k]
-        slot = (n + 4, 9 + 2 * n, 8 + 2 * n)[k]
-        return remote(kv.at[n], kv.at[slot], own_send.at[n * 3 + k], kv_recv.at[slot], device)
-
-    def fwd_copy(n):
-        late = lax.div(n, 24)
-        return remote(
-            kv.at[n], kv.at[n + 8 - 4 * late], fwd_send.at[n - 8 - 8 * late],
-            kv_recv.at[n + 8 - 4 * late], at(dc=1),
-        )
-
-    def hop_copy(n):
-        r = lax.div(n - 8, 2)
-        up = lax.rem(n, 2)
-        return remote(
-            kv.at[n], kv.at[24 + r], hop_send.at[r], kv_recv.at[24 + r], at(dy=3 - 2 * up)
+        slot = (own_slot(r) + 1, near_slot(r) + 1, near_slot(r))[k]
+        return remote(
+            kv.at[own_slot(r)], kv.at[slot], own_send.at[r * 3 + k], kv_recv.at[slot], device
+        )
+
+    def near_copy(r, k):
+        slot = near_slot(r) + k
+        return remote(
+            kv.at[slot], kv.at[slot + 2], fwd_send.at[r * 2 + k], kv_recv.at[slot + 2], at(dc=1)
+        )
+
+    def far_copy(r):
+        return remote(
+            kv.at[24 + r], kv.at[28 + r], fwd_send.at[8 + r], kv_recv.at[28 + r], at(dc=1)
+        )
+
+    def hop_copy(r):
+        up = 1 - lax.div(r, 2)
+        return remote(
+            kv.at[near_slot(r) + up], kv.at[24 + r], hop_send.at[r], kv_recv.at[24 + r],
+            at(dy=3 - 2 * up),
         )
 
     queries = dot(normed[...], wq[:, 0:512]) * Q_SCALE
@@ -294,63 +308,83 @@
     for d in (1, 3, 2):
         ow_copy(d).start()
 
-    def arrive(n):
-        remote(kv.at[n], kv.at[n], own_send.at[0], kv_recv.at[n], at(dc=1)).wait_recv()
-
-        @pl.when(n < 4)
+    def landed(slot):
+        remote(
+            kv.at[slot], kv.at[slot], own_send.at[0], kv_recv.at[slot], at(dc=1)
+        ).wait_recv()
+
+    def arrive(step, _):
+        landed(2 * step)
+
+        @pl.when(jnp.logical_and(step >= 3, step < 6))
         def _():
             for k in range(3):
-                own_copy(n, k).start()
-
-        near = jnp.logical_and(n >= 8, n < 16)
-
-        @pl.when(jnp.logical_and(near, lax.rem(n, 2) == jnp.where(n < 12, 1, 0)))
-        def _():
-            hop_copy(n).start()
-
-        @pl.when(jnp.logical_or(near, jnp.logical_and(n >= 24, n < 28)))
-        def _():
-            fwd_copy(n).start()
+                own_copy(step - 2, k).start()
+
+        landed(2 * step + 1)
+        late = jnp.logical_and(jnp.logical_and(step >= 6, step < 12), lax.rem(step, 2) == 0)
+
+        @pl.when(jnp.logical_or(step == 1, late))
+        def _():
+            r = jnp.where(step == 1, 0, lax.div(step, 2) - 2)
+            hop_copy(r).start()
+            near_copy(r, 0).start()
+            near_copy(r, 1).start()
+
+        @pl.when(jnp.logical_or(step == 12, step == 13))
+        def _():
+            far_copy(2 * (step - 12)).start()
+            far_copy(2 * (step - 12) + 1).start()
+
+        return 0
 
     for r in range(3):
         remote(q_buf.at[3], q_buf.at[2 - r], q_send.at[0], q_recv.at[r], at(dx=1)).wait_recv()
     acc[...] = jnp.zeros_like(acc)
     mref[...] = jnp.full_like(mref, -1e30)
-    tiles = (s0, s1)
-    ones = jnp.ones((16, 512), BF)
-
-    def logits(n, t, slot):
-        s = lax.dot_general(kv[n, 0:512, :], q_buf[t], NT, preferred_element_type=F32)
-        tiles[slot][...] = s
+    ones = jnp.ones((16, 1024), BF)
+    landed(1)
+
+    def logits(step, t, slot):
+        keys = jnp.concatenate([kv[2 * step, 0:512, :], kv[2 * step + 1, 0:512, :]], axis=0)
+        s = lax.dot_general(keys, q_buf[t], NT, preferred_element_type=F32)
+        (s0, s1)[slot][...] = s
         return jnp.max(s, axis=0, keepdims=True)
 
-    def fold(n, t, slot, block_max):
+    def weigh(t, slot, block_max):
         old = mref[t, 0:1, :]
         new = jnp.maximum(old, block_max)
         mref[t, 0:1, :] = new
-        p = jnp.exp2(tiles[slot][...] - new).astype(BF)
-        vt = jnp.concatenate([kv[n, 512 + j * 128 : 640 + j * 128, :] for j in range(4)], axis=1)
-        vt = jnp.concatenate([vt, ones], axis=0)
-        acc[t] = acc[t] * jnp.exp2(old - new) + dot(vt, p)
-
-    first = logits(0, 0, 0)
-
-    def block_step(n, block_max):
-        arrive(n + 1)
+        (p0, p1)[slot][...] = jnp.exp2((s0, s1)[slot][...] - new).astype(BF)
+        return jnp.exp2(old - new)
+
+    def add(step, t, slot, rescale):
+        pieces = [
+            kv[2 * step + i, 512 + j * 128 : 640 + j * 128, :] for i in range(2) for j in range(4)
+        ]
+        vt = jnp.concatenate([jnp.concatenate(pieces, axis=1), ones], axis=0)
+        acc[t] = acc[t] * rescale + dot(vt, (p0, p1)[slot][...])
+
+    def turns(units, state):
+        block_max, rescale = state
         for u in range(4):
-            ahead = n if u < 3 else n + 1
-            following = logits(ahead, (u + 1) % 4, (u + 1) % 2)
-            fold(n, u, u % 2, block_max)
-            block_max = following
-        return block_max
-
-    carry = lax.fori_loop(0, EARLY, block_step, first)
-
-    def arrive_late(n, _):
-        arrive(n)
-        return 0
-
-    lax.fori_loop(EARLY + 1, 32, arrive_late, 0)
+            following = logits(*units[u + 2], u % 2)
+            next_rescale = weigh(units[u + 1][1], (u + 1) % 2, block_max)
+            add(*units[u], u % 2, rescale)
+            block_max, rescale = following, next_rescale
+        return block_max, rescale
+
+    first = weigh(0, 0, logits(0, 0, 0))
+    state = (logits(0, 1, 1), first)
+
+    def by_step(step, state):
+        last = step == EARLY - 1
+        lax.fori_loop(step + 1, jnp.where(last, 16, step + 2), arrive, 0)
+        units = [(step, 0), (step, 1), (step, 2), (step, 3), (step + 1, 0)]
+        units.append((jnp.where(last, step + 2, step + 1), jnp.where(last, 0, 1)))
+        return turns(units, state)
+
+    state = lax.fori_loop(0, EARLY, by_step, state)
 
     mine = z * 4 + x
 
@@ -390,24 +424,10 @@
         head = z * 4 + lax.rem(x + order(3 - t), 4)
         remote(stage.at[0], att.at[head], ax_send.at[0], ax_recv.at[t], at(dx=1)).wait_recv()
 
-    def tile_step(t, block_max):
-        def group(i, block_max):
-            base = EARLY + i * 4
-            last = i == (32 - EARLY) // 4 - 1
-            for u in range(4):
-                if u < 3:
-                    following = logits(base + u + 1, t, (u + 1) % 2)
-                else:
-                    following = logits(
-                        jnp.where(last, EARLY, base + 4),
-                        jnp.where(last, jnp.minimum(t + 1, 3), t),
-                        0,
-                    )
-                fold(base + u, t, u % 2, block_max)
-                block_max = following
-            return block_max
-
-        block_max = lax.fori_loop(0, (32 - EARLY) // 4, group, block_max)
+    def by_tile(t, state):
+        after = jnp.minimum(t + 1, 3)
+        units = [(EARLY + i, t) for i in range(4)] + [(EARLY, after), (EARLY + 1, after)]
+        state = turns(units, state)
         a = acc[t]
         block = (a[0:128] / a[128:129]).T.astype(BF)
 
@@ -430,9 +450,9 @@
         def _():
             relay(t - 2)
 
-        return block_max
-
-    lax.fori_loop(0, 4, tile_step, carry)
+        return state
+
+    lax.fori_loop(0, 4, by_tile, state)
 
     def branch(dz):
         zs = lax.rem(z + dz, 4)
@@ -468,16 +488,13 @@
             own_copy(n, k).wait_send()
         for i in range(4):
             az_copy(n, i).wait_send()
-        hop_copy(9 + 2 * n - lax.div(n, 2)).wait_send()
+        hop_copy(n).wait_send()
+        near_copy(n, 0).wait_send()
+        near_copy(n, 1).wait_send()
+        far_copy(n).wait_send()
         return 0
 
     lax.fori_loop(0, 4, drain, 0)
-
-    def drain_fwd(i, _):
-        fwd_copy(8 + i + 8 * lax.div(i, 8)).wait_send()
-        return 0
-
-    lax.fori_loop(0, 12, drain_fwd, 0)
 
 
 def on_device(tokens, key_query, value_weight, proj_weight, norm_gain, qkv_weight, out_weight):
@@ -492,7 +509,7 @@
         vm((2, 1536, 128), BF),
         vm((1536, 128), F32),
         vm((2048, 1536), BF),
-        vm((NV * CH, 128), BF),
+        vm((NV * CH, 128), F32),
         vm((4, CH, 1024), BF),
         vm((3, CH, 1024), BF),
         vm((4, CH, 128), F32),
@@ -504,8 +521,10 @@
         vm((4, 2 * ROWS, 128), BF),
         vm((4, ROWS, 128), BF),
         vm((32, 2 * ROWS, 128), BF),
-        vm((512, 512), F32),
-        vm((512, 512), F32),
+        vm((1024, 512), F32),
+        vm((1024, 512), F32),
+        vm((1024, 512), BF),
+        vm((1024, 512), BF),
         vm((4, 144, 512), F32),
         vm((4, 8, 512), F32),
         vm((4, 512, 512), BF),

time: 135 us -> 133 us (0.985)
  Pallas kernels: 133 us -> 131 us
    pallas_call x1, Pallas kernels: 133 us -> 131 us  [on_device(): pl.pallas_call(kernel, out_shape=jax.ShapeDtypeStruct((ROWS, 512), BF), i...]
where the time goes in v4:
time: 133 us; the launch traced here: 132 us
  Pallas kernels  131 us (98%)
  local copies, waits for them, and re-layouts  1.87 us (1%)
    pallas_call x1, Pallas kernels, on_device(): pl.pallas_call(kernel, out_shape=jax.ShapeDtypeStruct((ROWS, 512), BF), i...  131 us

profile of v4, /device:TPU:0, one launch (start us, length us, event | category | flops | bytes accessed | tf_op | source)
XLA Modules:
  0.0 132.4 jit_solution(2269694834255414391)
XLA Ops:
  0.0 130.5 %block.1 = bf16[512,512]{1,0:T(8,128)(2,1)} custom-call(bf16[12,512,1024]{2,1,0:T(8,128)(2,1)} %tok_hbm.1, bf16[16,1024]{1,0:T(8,128)(2,1)} %bitcast.6, bf16[1024,1024]{1,0:T(8,128)(2,1)} %vw_hbm.1, bf16[1024,2048]{1,0:T(8,128)(2,1)} %proj_hbm.1, f32[1,2048]{1,0:T(1,128)} %bitcast.7, bf16[24576,128]{1,0:T(8,128)(2,1)} %bitcast.4, bf16[512,2048]{1,0:T(8,128)(2,1)} %bitcast.5), custom_call_target="tpu_custom_call" | custom-call | tf_op jit(solution)/shard_map/block/pallas_call | solution.py:540
  130.6 1.9 %copy.9 = bf16[512,512]{1,0:T(8,128)(2,1)} copy(bf16[512,512]{1,0:T(8,128)(2,1)} %block.1) | data formatting | bytes 1048576

commit v5 on v4

--- a/solution.py
+++ b/solution.py
@@ -13,7 +13,6 @@
 F32 = jnp.float32
 
 ROWS, NV, CH = 512, 12, 128
-EARLY = 12
 Q_SCALE = 128 ** (-0.5) * 1.4426950408889634
 
 
@@ -33,10 +32,12 @@
     tok, kqp, expand, vw, proj, wstage, wf, wq,
     wn, part_send, part_recv, stat_send, stat_recv, pooled,
     emb, normed, q4, kv4, q_buf, kv, s0, s1, p0, p1, acc, mref,
+    res_send, res_recv, scale_send, scale_recv,
     ow, stage, att,
     sem_tok, sem_w, sem_w2, sem_ow_own,
     ps_send, ps_recv, st_send, st_recv, pool_send, pool_recv,
-    q_send, q_recv, kvx_send, own_send, fwd_send, hop_send, kv_recv,
+    q_send, q_recv, kvx_send, own_send, fwd_send, kv_recv,
+    mate_send, mate_recv, rs_send, rs_recv, ss_send, ss_recv,
     ow_send, ow_recv, ax_send, ax_recv, az_send, az_recv,
 ):
     z = lax.axis_index("var")
@@ -234,43 +235,33 @@
         slot = own_slot(dst)
         return remote(kv4.at[head], kv.at[slot], kvx_send.at[d - 1], kv_recv.at[slot], at(dx=d))
 
+    odd = lax.rem(y, 2)
+    partner = at(dy=1 + 2 * odd)
+    mate = at(dy=3 - 2 * odd)
+
     def own_slot(r):
-        return (0, 6, 8, 10)[r] if isinstance(r, int) else jnp.where(r == 0, 0, 4 + 2 * r)
-
-    def near_slot(r):
-        return (2, 12, 16, 20)[r] if isinstance(r, int) else jnp.where(r == 0, 2, 8 + 4 * r)
+        return (0, 4, 6, 8)[r] if isinstance(r, int) else jnp.where(r == 0, 0, 2 + 2 * r)
+
+    def pair_slot(r):
+        return (2, 10, 12, 14)[r] if isinstance(r, int) else jnp.where(r == 0, 2, 8 + 2 * r)
 
     def own_copy(r, k):
-        device = (at(dc=1), at(dy=1), at(dy=3))[k]
-        slot = (own_slot(r) + 1, near_slot(r) + 1, near_slot(r))[k]
-        return remote(
-            kv.at[own_slot(r)], kv.at[slot], own_send.at[r * 3 + k], kv_recv.at[slot], device
-        )
-
-    def near_copy(r, k):
-        slot = near_slot(r) + k
-        return remote(
-            kv.at[slot], kv.at[slot + 2], fwd_send.at[r * 2 + k], kv_recv.at[slot + 2], at(dc=1)
-        )
-
-    def far_copy(r):
-        return remote(
-            kv.at[24 + r], kv.at[28 + r], fwd_send.at[8 + r], kv_recv.at[28 + r], at(dc=1)
-        )
-
-    def hop_copy(r):
-        up = 1 - lax.div(r, 2)
-        return remote(
-            kv.at[near_slot(r) + up], kv.at[24 + r], hop_send.at[r], kv_recv.at[24 + r],
-            at(dy=3 - 2 * up),
-        )
-
-    queries = dot(normed[...], wq[:, 0:512]) * Q_SCALE
-    for h in range(4):
-        q4[h] = queries[:, h * 128 : (h + 1) * 128].astype(BF)
-    for d in (2, 1, 3):
-        q_copy(d).start()
-    q_buf[3] = q4[x]
+        slot = (own_slot(r) + 1, pair_slot(r))[k]
+        return remote(
+            kv.at[own_slot(r)], kv.at[slot], own_send.at[r * 2 + k], kv_recv.at[slot],
+            (at(dc=1), partner)[k],
+        )
+
+    def pair_copy(r):
+        slot = pair_slot(r)
+        return remote(
+            kv.at[slot], kv.at[slot + 1], fwd_send.at[r], kv_recv.at[slot + 1], at(dc=1)
+        )
+
+    def mate_copy(r):
+        return remote(
+            q_buf.at[3 - r], q_buf.at[4 + r], mate_send.at[r], mate_recv.at[r], mate
+        )
 
     def keys_values(head, write):
         cs = pl.ds(pl.multiple_of(512 + head * 256, 256), 256)
@@ -284,8 +275,15 @@
         kv[0, rows, :] = value
 
     keys_values(x, write_own)
-    for k in range(3):
-        own_copy(0, k).start()
+    own_copy(0, 0).start()
+    own_copy(0, 1).start()
+    queries = dot(normed[...], wq[:, 0:512]) * Q_SCALE
+    for h in range(4):
+        q4[h] = queries[:, h * 128 : (h + 1) * 128].astype(BF)
+    for d in (1, 3, 2):
+        q_copy(d).start()
+    q_buf[3] = q4[x]
+    mate_copy(0).start()
     for d in (1, 3, 2):
         head = lax.rem(x + d, 4)
 
@@ -313,33 +311,32 @@
             kv.at[slot], kv.at[slot], own_send.at[0], kv_recv.at[slot], at(dc=1)
         ).wait_recv()
 
-    def arrive(step, _):
+    def arrive(step):
         landed(2 * step)
-
-        @pl.when(jnp.logical_and(step >= 3, step < 6))
-        def _():
-            for k in range(3):
-                own_copy(step - 2, k).start()
+        own = jnp.logical_and(step >= 2, step < 5)
+
+        @pl.when(own)
+        def _():
+            own_copy(step - 1, 0).start()
+            own_copy(step - 1, 1).start()
+
+        @pl.when(jnp.logical_not(own))
+        def _():
+            pair_copy(jnp.where(step == 1, 0, step - 4)).start()
 
         landed(2 * step + 1)
-        late = jnp.logical_and(jnp.logical_and(step >= 6, step < 12), lax.rem(step, 2) == 0)
-
-        @pl.when(jnp.logical_or(step == 1, late))
-        def _():
-            r = jnp.where(step == 1, 0, lax.div(step, 2) - 2)
-            hop_copy(r).start()
-            near_copy(r, 0).start()
-            near_copy(r, 1).start()
-
-        @pl.when(jnp.logical_or(step == 12, step == 13))
-        def _():
-            far_copy(2 * (step - 12)).start()
-            far_copy(2 * (step - 12) + 1).start()
-
-        return 0
-
-    for r in range(3):
-        remote(q_buf.at[3], q_buf.at[2 - r], q_send.at[0], q_recv.at[r], at(dx=1)).wait_recv()
+
+    for r in (1, 2, 3):
+        remote(
+            q_buf.at[3], q_buf.at[3 - r], q_send.at[0], q_recv.at[r - 1], at(dx=1)
+        ).wait_recv()
+        mate_copy(r).start()
+
+    def mate_arrive(r):
+        remote(
+            q_buf.at[0], q_buf.at[4 + r], mate_send.at[0], mate_recv.at[r], mate
+        ).wait_recv()
+
     acc[...] = jnp.zeros_like(acc)
     mref[...] = jnp.full_like(mref, -1e30)
     ones = jnp.ones((16, 1024), BF)
@@ -377,14 +374,35 @@
     first = weigh(0, 0, logits(0, 0, 0))
     state = (logits(0, 1, 1), first)
 
-    def by_step(step, state):
-        last = step == EARLY - 1
-        lax.fori_loop(step + 1, jnp.where(last, 16, step + 2), arrive, 0)
-        units = [(step, 0), (step, 1), (step, 2), (step, 3), (step + 1, 0)]
-        units.append((jnp.where(last, step + 2, step + 1), jnp.where(last, 0, 1)))
+    def place_of(k):
+        step = jnp.where(k < 4, lax.rem(k, 2), lax.div(k, 2))
+        group = jnp.where(k < 4, lax.div(k, 2), lax.rem(k, 2))
+        return step, 4 * group
+
+    def by_step(k, state):
+        @pl.when(k == 0)
+        def _():
+            arrive(1)
+
+        @pl.when(jnp.logical_or(k == 1, k == 2))
+        def _():
+            arrive(k + 1)
+            mate_arrive(2 * k - 2)
+            mate_arrive(2 * k - 1)
+
+        @pl.when(k >= 4)
+        def _():
+            arrive(k)
+
+        step, tile = place_of(k)
+        next_step, next_tile = place_of(k + 1)
+        last = k == 7
+        units = [(step, tile + u) for u in range(4)]
+        units.append((next_step, jnp.where(last, 7, next_tile)))
+        units.append((jnp.where(last, 5, next_step), jnp.where(last, 7, next_tile + 1)))
         return turns(units, state)
 
-    state = lax.fori_loop(0, EARLY, by_step, state)
+    state = lax.fori_loop(0, 8, by_step, state)
 
     mine = z * 4 + x
 
@@ -424,35 +442,76 @@
         head = z * 4 + lax.rem(x + order(3 - t), 4)
         remote(stage.at[0], att.at[head], ax_send.at[0], ax_recv.at[t], at(dx=1)).wait_recv()
 
-    def by_tile(t, state):
-        after = jnp.minimum(t + 1, 3)
-        units = [(EARLY + i, t) for i in range(4)] + [(EARLY, after), (EARLY + 1, after)]
+    def result_copy(r):
+        return remote(
+            res_send.at[r], res_recv.at[r], rs_send.at[r], rs_recv.at[r], mate
+        )
+
+    def scale_copy(r):
+        return remote(
+            scale_send.at[r], scale_recv.at[r], ss_send.at[r], ss_recv.at[r], mate
+        )
+
+    def tile_of(i):
+        return jnp.where(i < 4, 7 - i, i - 4)
+
+    def by_tile(i, state):
+        tile = tile_of(i)
+        after = tile_of(jnp.minimum(i + 1, 7))
+        units = [(4 + j, tile) for j in range(4)] + [(4, after), (5, after)]
         state = turns(units, state)
-        a = acc[t]
-        block = (a[0:128] / a[128:129]).T.astype(BF)
-
-        @pl.when(t < 3)
-        def _():
-            stage[t] = block
-            ax_copy(t).start()
-
-        @pl.when(t == 3)
-        def _():
-            att[mine] = block
-            share(3)
-
-        @pl.when(t > 0)
-        def _():
-            ax_arrive(t - 1)
-            share(t - 1)
-
-        @pl.when(t > 1)
-        def _():
-            relay(t - 2)
+
+        @pl.when(i < 4)
+        def _():
+            r = 3 - i
+            total = acc[tile, 128:129, :]
+            res_send[r] = (acc[tile, 0:128, :] / total).astype(BF)
+            scale_send[r, 0:1, :] = mref[tile, 0:1, :]
+            scale_send[r, 1:2, :] = total
+            result_copy(r).start()
+            scale_copy(r).start()
+
+        @pl.when(i >= 4)
+        def _():
+            t = i - 4
+            r = 3 - t
+            remote(
+                res_send.at[0], res_recv.at[r], rs_send.at[0], rs_recv.at[r], mate
+            ).wait_recv()
+            remote(
+                scale_send.at[0], scale_recv.at[r], ss_send.at[0], ss_recv.at[r], mate
+            ).wait_recv()
+            here, there = mref[tile, 0:1, :], scale_recv[r, 0:1, :]
+            high = jnp.maximum(here, there)
+            here = jnp.exp2(here - high)
+            there = jnp.exp2(there - high) * scale_recv[r, 1:2, :]
+            inverse = 1.0 / (here * acc[tile, 128:129, :] + there)
+            both = acc[tile, 0:128, :] * (here * inverse)
+            both = both + res_recv[r].astype(F32) * (there * inverse)
+            block = both.T.astype(BF)
+
+            @pl.when(t < 3)
+            def _():
+                stage[t] = block
+                ax_copy(t).start()
+
+            @pl.when(t == 3)
+            def _():
+                att[mine] = block
+                share(3)
+
+            @pl.when(t > 0)
+            def _():
+                ax_arrive(t - 1)
+                share(t - 1)
+
+            @pl.when(t > 1)
+            def _():
+                relay(t - 2)
 
         return state
 
-    lax.fori_loop(0, 4, by_tile, state)
+    lax.fori_loop(0, 8, by_tile, state)
 
     def branch(dz):
         zs = lax.rem(z + dz, 4)
@@ -484,14 +543,14 @@
         ax_copy(d - 1).wait_send()
 
     def drain(n, _):
-        for k in range(3):
+        for k in range(2):
             own_copy(n, k).wait_send()
+        pair_copy(n).wait_send()
+        mate_copy(n).wait_send()
+        result_copy(n).wait_send()
+        scale_copy(n).wait_send()
         for i in range(4):
             az_copy(n, i).wait_send()
-        hop_copy(n).wait_send()
-        near_copy(n, 0).wait_send()
-        near_copy(n, 1).wait_send()
-        far_copy(n).wait_send()
         return 0
 
     lax.fori_loop(0, 4, drain, 0)
@@ -519,20 +578,25 @@
         vm((ROWS, 2048), BF),
         vm((4, ROWS, 128), BF),
         vm((4, 2 * ROWS, 128), BF),
-        vm((4, ROWS, 128), BF),
-        vm((32, 2 * ROWS, 128), BF),
+        vm((8, ROWS, 128), BF),
+        vm((16, 2 * ROWS, 128), BF),
         vm((1024, 512), F32),
         vm((1024, 512), F32),
         vm((1024, 512), BF),
         vm((1024, 512), BF),
-        vm((4, 144, 512), F32),
+        vm((8, 144, 512), F32),
+        vm((8, 8, 512), F32),
+        vm((4, 128, 512), BF),
+        vm((4, 128, 512), BF),
+        vm((4, 8, 512), F32),
         vm((4, 8, 512), F32),
         vm((4, 512, 512), BF),
         vm((3, ROWS, 128), BF),
         vm((16, ROWS, 128), BF),
         dma((2,)), dma((2,)), dma((2,)), dma,
         dma((3,)), dma((3,)), dma((3,)), dma((3,)), dma((4,)), dma((4,)),
-        dma((3,)), dma((3,)), dma((3,)), dma((12,)), dma((12,)), dma((4,)), dma((32,)),
+        dma((3,)), dma((3,)), dma((3,)), dma((8,)), dma((4,)), dma((16,)),
+        dma((4,)), dma((4,)), dma((4,)), dma((4,)), dma((4,)), dma((4,)),
         dma((3,)), dma((3,)), dma((3,)), dma((3,)), dma((16,)), dma((16,)),
     ]
     anywhere = pl.BlockSpec(memory_space=pl.ANY)

time: 133 us -> 135 us (1.015)
  Pallas kernels: 131 us -> 133 us
    pallas_call x1, Pallas kernels: 131 us -> 133 us  [on_device(): pl.pallas_call(kernel, out_shape=jax.ShapeDtypeStruct((ROWS, 512), BF), i...]
where the time goes in v5:
time: 135 us
  Pallas kernels  133 us (99%)
  local copies, waits for them, and re-layouts  1.87 us (1%)
    pallas_call x1, Pallas kernels, on_device(): pl.pallas_call(kernel, out_shape=jax.ShapeDtypeStruct((ROWS, 512), BF), i...  133 us

profile of v5, /device:TPU:0, one launch (start us, length us, event | category | flops | bytes accessed | tf_op | source)
XLA Modules:
  0.0 134.7 jit_solution(1624545551602836079)
XLA Ops:
  0.0 132.9 %block.1 = bf16[512,512]{1,0:T(8,128)(2,1)} custom-call(bf16[12,512,1024]{2,1,0:T(8,128)(2,1)} %tok_hbm.1, bf16[16,1024]{1,0:T(8,128)(2,1)} %bitcast.6, bf16[1024,1024]{1,0:T(8,128)(2,1)} %vw_hbm.1, bf16[1024,2048]{1,0:T(8,128)(2,1)} %proj_hbm.1, f32[1,2048]{1,0:T(1,128)} %bitcast.7, bf16[24576,128]{1,0:T(8,128)(2,1)} %bitcast.4, bf16[512,2048]{1,0:T(8,128)(2,1)} %bitcast.5), custom_call_target="tpu_custom_call" | custom-call | tf_op jit(solution)/shard_map/block/pallas_call | solution.py:604
  132.9 1.9 %copy.9 = bf16[512,512]{1,0:T(8,128)(2,1)} copy(bf16[512,512]{1,0:T(8,128)(2,1)} %block.1) | data formatting | bytes 1048576

commit v6 on v5

--- a/solution.py
+++ b/solution.py
@@ -291,7 +291,8 @@
             kv4[head, rows, :] = value
 
         keys_values(head, write_other)
-        kvx_copy(d).start()
+        if d != 2:
+            kvx_copy(d).start()
 
     my_cols = pl.ds(pl.multiple_of(z * 512, 512), 512)
     ow_own = pltpu.make_async_copy(ow_hbm.at[:, my_cols], ow.at[z], sem_ow_own)
@@ -312,7 +313,10 @@
         ).wait_recv()
 
     def arrive(step):
-        landed(2 * step)
+        @pl.when(step != 2)
+        def _():
+            landed(2 * step)
+
         own = jnp.logical_and(step >= 2, step < 5)
 
         @pl.when(own)
@@ -384,6 +388,11 @@
         def _():
             arrive(1)
 
+        @pl.when(k == 1)
+        def _():
+            landed(own_slot(1))
+            kvx_copy(2).start()
+
         @pl.when(jnp.logical_or(k == 1, k == 2))
         def _():
             arrive(k + 1)
@@ -453,7 +462,8 @@
         )
 
     def tile_of(i):
-        return jnp.where(i < 4, 7 - i, i - 4)
+        inner = jnp.where(lax.rem(i, 2) == 1, 6 - lax.div(i, 2), lax.div(i, 2) - 1)
+        return jnp.where(i == 0, 7, jnp.where(i == 7, 3, inner))
 
     def by_tile(i, state):
         tile = tile_of(i)
@@ -461,9 +471,9 @@
         units = [(4 + j, tile) for j in range(4)] + [(4, after), (5, after)]
         state = turns(units, state)
 
-        @pl.when(i < 4)
-        def _():
-            r = 3 - i
+        @pl.when(tile >= 4)
+        def _():
+            r = tile - 4
             total = acc[tile, 128:129, :]
             res_send[r] = (acc[tile, 0:128, :] / total).astype(BF)
             scale_send[r, 0:1, :] = mref[tile, 0:1, :]
@@ -471,9 +481,9 @@
             result_copy(r).start()
             scale_copy(r).start()
 
-        @pl.when(i >= 4)
-        def _():
-            t = i - 4
+        @pl.when(tile < 4)
+        def _():
+            t = tile
             r = 3 - t
             remote(
                 res_send.at[0], res_recv.at[r], rs_send.at[0], rs_recv.at[r], mate
@@ -500,14 +510,16 @@
                 att[mine] = block
                 share(3)
 
-            @pl.when(t > 0)
-            def _():
-                ax_arrive(t - 1)
-                share(t - 1)
-
-            @pl.when(t > 1)
-            def _():
-                relay(t - 2)
+        @pl.when(i == 4)
+        def _():
+            ax_arrive(0)
+            share(0)
+
+        @pl.when(i == 6)
+        def _():
+            ax_arrive(1)
+            share(1)
+            relay(0)
 
         return state
 
@@ -522,12 +534,15 @@
         src = lax.rem(z + d, 4)
         remote(ow.at[src], ow.at[src], ow_send.at[0], ow_recv.at[d - 1], at(dz=1)).wait_recv()
 
+    ax_arrive(2)
+    share(2)
+    relay(1)
     ow_own.wait()
     for d in (1, 2, 3):
         ow_arrive(d)
     result = emb[:, my_cols] + branch(0)
+    relay(3)
     relay(2)
-    relay(3)
     result = result + branch(1) + branch(3)
     for t in range(4):
         az_arrive(t, 2)

time: 135 us -> 134 us (level)
  Pallas kernels: 133 us -> 131 us
    pallas_call x1, Pallas kernels: 133 us -> 131 us  [on_device(): pl.pallas_call(kernel, out_shape=jax.ShapeDtypeStruct((ROWS, 512), BF), i...]
where the time goes in v6:
time: 134 us; the launch traced here: 133 us
  Pallas kernels  131 us (98%)
  local copies, waits for them, and re-layouts  1.87 us (1%)
    pallas_call x1, Pallas kernels, on_device(): pl.pallas_call(kernel, out_shape=jax.ShapeDtypeStruct((ROWS, 512), BF), i...  131 us

profile of v6, /device:TPU:0, one launch (start us, length us, event | category | flops | bytes accessed | tf_op | source)
XLA Modules:
  0.0 133.3 jit_solution(12180448247211022326)
XLA Ops:
  0.0 131.4 %block.1 = bf16[512,512]{1,0:T(8,128)(2,1)} custom-call(bf16[12,512,1024]{2,1,0:T(8,128)(2,1)} %tok_hbm.1, bf16[16,1024]{1,0:T(8,128)(2,1)} %bitcast.6, bf16[1024,1024]{1,0:T(8,128)(2,1)} %vw_hbm.1, bf16[1024,2048]{1,0:T(8,128)(2,1)} %proj_hbm.1, f32[1,2048]{1,0:T(1,128)} %bitcast.7, bf16[24576,128]{1,0:T(8,128)(2,1)} %bitcast.4, bf16[512,2048]{1,0:T(8,128)(2,1)} %bitcast.5), custom_call_target="tpu_custom_call" | custom-call | tf_op jit(solution)/shard_map/block/pallas_call | solution.py:619
  131.4 1.9 %copy.9 = bf16[512,512]{1,0:T(8,128)(2,1)} copy(bf16[512,512]{1,0:T(8,128)(2,1)} %block.1) | data formatting | bytes 1048576

commit v7 on v6

--- a/solution.py
+++ b/solution.py
@@ -312,22 +312,15 @@
             kv.at[slot], kv.at[slot], own_send.at[0], kv_recv.at[slot], at(dc=1)
         ).wait_recv()
 
-    def arrive(step):
-        @pl.when(step != 2)
-        def _():
-            landed(2 * step)
-
-        own = jnp.logical_and(step >= 2, step < 5)
-
-        @pl.when(own)
-        def _():
+    def bring(step):
+        landed(2 * step)
+        if step in (2, 3, 4):
             own_copy(step - 1, 0).start()
             own_copy(step - 1, 1).start()
-
-        @pl.when(jnp.logical_not(own))
-        def _():
-            pair_copy(jnp.where(step == 1, 0, step - 4)).start()
-
+        else:
+            pair_copy(0 if step == 1 else step - 4).start()
+
+    def ready(step):
         landed(2 * step + 1)
 
     for r in (1, 2, 3):
@@ -386,22 +379,43 @@
     def by_step(k, state):
         @pl.when(k == 0)
         def _():
-            arrive(1)
+            ready(1)
 
         @pl.when(k == 1)
         def _():
-            landed(own_slot(1))
+            bring(2)
             kvx_copy(2).start()
-
-        @pl.when(jnp.logical_or(k == 1, k == 2))
-        def _():
-            arrive(k + 1)
-            mate_arrive(2 * k - 2)
-            mate_arrive(2 * k - 1)
-
-        @pl.when(k >= 4)
-        def _():
-            arrive(k)
+            bring(3)
+            mate_arrive(0)
+            mate_arrive(1)
+
+        @pl.when(k == 2)
+        def _():
+            mate_arrive(2)
+            mate_arrive(3)
+
+        @pl.when(k == 3)
+        def _():
+            ready(2)
+
+        @pl.when(k == 4)
+        def _():
+            bring(4)
+
+        @pl.when(k == 5)
+        def _():
+            ready(3)
+            bring(5)
+
+        @pl.when(k == 6)
+        def _():
+            ready(4)
+            bring(6)
+
+        @pl.when(k == 7)
+        def _():
+            ready(5)
+            bring(7)
 
         step, tile = place_of(k)
         next_step, next_tile = place_of(k + 1)
@@ -411,7 +425,10 @@
         units.append((jnp.where(last, 5, next_step), jnp.where(last, 7, next_tile + 1)))
         return turns(units, state)
 
+    bring(1)
     state = lax.fori_loop(0, 8, by_step, state)
+    ready(6)
+    ready(7)
 
     mine = z * 4 + x
 

time: 134 us -> 128 us (0.955)
  Pallas kernels: 131 us -> 126 us
    pallas_call x1, Pallas kernels: 131 us -> 126 us  [on_device(): pl.pallas_call(kernel, out_shape=jax.ShapeDtypeStruct((ROWS, 512), BF), i...]
where the time goes in v7:
time: 128 us
  Pallas kernels  126 us (98%)
  local copies, waits for them, and re-layouts  1.87 us (1%)
    pallas_call x1, Pallas kernels, on_device(): pl.pallas_call(kernel, out_shape=jax.ShapeDtypeStruct((ROWS, 512), BF), i...  126 us

profile of v7, /device:TPU:0, one launch (start us, length us, event | category | flops | bytes accessed | tf_op | source)
XLA Modules:
  0.0 128.1 jit_solution(14244206168860764512)
XLA Ops:
  0.0 126.2 %block.1 = bf16[512,512]{1,0:T(8,128)(2,1)} custom-call(bf16[12,512,1024]{2,1,0:T(8,128)(2,1)} %tok_hbm.1, bf16[16,1024]{1,0:T(8,128)(2,1)} %bitcast.6, bf16[1024,1024]{1,0:T(8,128)(2,1)} %vw_hbm.1, bf16[1024,2048]{1,0:T(8,128)(2,1)} %proj_hbm.1, f32[1,2048]{1,0:T(1,128)} %bitcast.7, bf16[24576,128]{1,0:T(8,128)(2,1)} %bitcast.4, bf16[512,2048]{1,0:T(8,128)(2,1)} %bitcast.5), custom_call_target="tpu_custom_call" | custom-call | tf_op jit(solution)/shard_map/block/pallas_call | solution.py:636
  126.2 1.9 %copy.9 = bf16[512,512]{1,0:T(8,128)(2,1)} copy(bf16[512,512]{1,0:T(8,128)(2,1)} %block.1) | data formatting | bytes 1048576

commit v8 on v7

--- a/solution.py
+++ b/solution.py
@@ -116,7 +116,7 @@
         weights = jnp.exp(scores - peak[None])
         totals = jnp.sum(weights, axis=0)
         first_lanes = lax.broadcasted_iota(jnp.int32, (CH, 128), 1) < 16
-        stat_send[j] = jnp.where(first_lanes, peak, pltpu.roll(totals, 16, 1))
+        stat_send[j] = jnp.where(first_lanes, peak, pltpu.roll(totals, 16, 1)).T[0:32, :]
         wn[...] = weights.astype(BF).astype(F32).reshape(NV * CH, 128)
 
         upper = jnp.where(lax.broadcasted_iota(jnp.int32, (NV * CH, 128), 1) >= 64, 1, 0)
@@ -148,7 +148,9 @@
         stat_copy(i).wait_send()
         remote(part_send.at[0], part_recv.at[i], ps_send.at[0], ps_recv.at[i], at(dz=1)).wait_recv()
         remote(stat_send.at[0], stat_recv.at[i], st_send.at[0], st_recv.at[i], at(dz=1)).wait_recv()
+    empty = jnp.zeros((96, 128), F32)
     peaks = [stat_send[3]] + [stat_recv[i] for i in range(3)]
+    peaks = [jnp.concatenate([p, empty], axis=0).T for p in peaks]
     top = functools.reduce(jnp.maximum, peaks)
     factors = [jnp.exp(l - top) for l in peaks]
     inverse = 1.0 / sum(f * pltpu.roll(l, 112, 1) for f, l in zip(factors, peaks))
@@ -274,16 +276,16 @@
     def write_own(rows, value):
         kv[0, rows, :] = value
 
+    queries = dot(normed[...], wq[:, 0:512]) * Q_SCALE
+    for h in range(4):
+        q4[h] = queries[:, h * 128 : (h + 1) * 128].astype(BF)
+    for d in (2, 1, 3):
+        q_copy(d).start()
+    q_buf[3] = q4[x]
+    mate_copy(0).start()
     keys_values(x, write_own)
     own_copy(0, 0).start()
     own_copy(0, 1).start()
-    queries = dot(normed[...], wq[:, 0:512]) * Q_SCALE
-    for h in range(4):
-        q4[h] = queries[:, h * 128 : (h + 1) * 128].astype(BF)
-    for d in (1, 3, 2):
-        q_copy(d).start()
-    q_buf[3] = q4[x]
-    mate_copy(0).start()
     for d in (1, 3, 2):
         head = lax.rem(x + d, 4)
 
@@ -328,6 +330,8 @@
             q_buf.at[3], q_buf.at[3 - r], q_send.at[0], q_recv.at[r - 1], at(dx=1)
         ).wait_recv()
         mate_copy(r).start()
+        if r == 2:
+            bring(1)
 
     def mate_arrive(r):
         remote(
@@ -385,12 +389,12 @@
         def _():
             bring(2)
             kvx_copy(2).start()
-            bring(3)
             mate_arrive(0)
             mate_arrive(1)
 
         @pl.when(k == 2)
         def _():
+            bring(3)
             mate_arrive(2)
             mate_arrive(3)
 
@@ -425,7 +429,6 @@
         units.append((jnp.where(last, 5, next_step), jnp.where(last, 7, next_tile + 1)))
         return turns(units, state)
 
-    bring(1)
     state = lax.fori_loop(0, 8, by_step, state)
     ready(6)
     ready(7)
@@ -603,8 +606,8 @@
         vm((NV * CH, 128), F32),
         vm((4, CH, 1024), BF),
         vm((3, CH, 1024), BF),
-        vm((4, CH, 128), F32),
-        vm((3, CH, 128), F32),
+        vm((4, 32, CH), F32),
+        vm((3, 32, CH), F32),
         vm((ROWS, 1024), BF),
         vm((ROWS, 2048), F32),
         vm((ROWS, 2048), BF),

time: 128 us -> 124 us (0.969)
  Pallas kernels: 126 us -> 122 us
    pallas_call x1, Pallas kernels: 126 us -> 122 us  [on_device(): pl.pallas_call(kernel, out_shape=jax.ShapeDtypeStruct((ROWS, 512), BF), i...]
where the time goes in v8:
time: 124 us; the launch traced here: 123 us
  Pallas kernels  122 us (98%)
  local copies, waits for them, and re-layouts  1.87 us (2%)
    pallas_call x1, Pallas kernels, on_device(): pl.pallas_call(kernel, out_shape=jax.ShapeDtypeStruct((ROWS, 512), BF), i...  122 us

profile of v8, /device:TPU:0, one launch (start us, length us, event | category | flops | bytes accessed | tf_op | source)
XLA Modules:
  0.0 123.5 jit_solution(4667400401985137105)
XLA Ops:
  0.0 121.6 %block.1 = bf16[512,512]{1,0:T(8,128)(2,1)} custom-call(bf16[12,512,1024]{2,1,0:T(8,128)(2,1)} %tok_hbm.1, bf16[16,1024]{1,0:T(8,128)(2,1)} %bitcast.6, bf16[1024,1024]{1,0:T(8,128)(2,1)} %vw_hbm.1, bf16[1024,2048]{1,0:T(8,128)(2,1)} %proj_hbm.1, f32[1,2048]{1,0:T(1,128)} %bitcast.7, bf16[24576,128]{1,0:T(8,128)(2,1)} %bitcast.4, bf16[512,2048]{1,0:T(8,128)(2,1)} %bitcast.5), custom_call_target="tpu_custom_call" | custom-call | tf_op jit(solution)/shard_map/block/pallas_call | solution.py:639
  121.6 1.9 %copy.9 = bf16[512,512]{1,0:T(8,128)(2,1)} copy(bf16[512,512]{1,0:T(8,128)(2,1)} %block.1) | data formatting | bytes 1048576

commit v9 on v8

--- a/solution.py
+++ b/solution.py
@@ -68,17 +68,12 @@
     proj_copy = pltpu.make_async_copy(proj_hbm, proj, sem_w.at[1])
     tok_copy(0, 0).start()
     vw_copy.start()
-    tok_copy(1, 1).start()
-    proj_copy.start()
 
     def w2_copy(i, slot):
         base = pl.multiple_of(i * 1536, 1536)
         return pltpu.make_async_copy(
             w2_hbm.at[pl.ds(base, 1536), :], wstage.at[slot], sem_w2.at[slot]
         )
-
-    w2_copy(0, 0).start()
-    w2_copy(1, 1).start()
 
     barrier = pltpu.get_barrier_semaphore()
     partners = [at(dx=d) for d in (1, 2, 3)] + [at(dy=d) for d in (1, 2, 3)]
@@ -109,6 +104,14 @@
     def pool_chunk(j, _):
         slot = lax.rem(j, 2)
         tok_copy(j, slot).wait()
+
+        @pl.when(j == 0)
+        def _():
+            tok_copy(1, 1).start()
+            proj_copy.start()
+            w2_copy(0, 0).start()
+            w2_copy(1, 1).start()
+
         scores = lax.dot_general(
             tok[slot].reshape(NV * CH, 1024), kqp[...], NT, preferred_element_type=F32
         ).reshape(NV, CH, 128)
@@ -208,11 +211,11 @@
         pool_arrive(i)
 
     def project(i, _):
-        cs = pl.ds(pl.multiple_of(i * 512, 512), 512)
+        cs = pl.ds(pl.multiple_of(i * 1024, 1024), 1024)
         emb[:, cs] = dot(pooled[...], proj[:, cs])
         return 0
 
-    lax.fori_loop(0, 4, project, 0)
+    lax.fori_loop(0, 2, project, 0)
 
     def norm(i, _):
         rows = pl.ds(pl.multiple_of(i * 128, 128), 128)
@@ -325,14 +328,6 @@
     def ready(step):
         landed(2 * step + 1)
 
-    for r in (1, 2, 3):
-        remote(
-            q_buf.at[3], q_buf.at[3 - r], q_send.at[0], q_recv.at[r - 1], at(dx=1)
-        ).wait_recv()
-        mate_copy(r).start()
-        if r == 2:
-            bring(1)
-
     def mate_arrive(r):
         remote(
             q_buf.at[0], q_buf.at[4 + r], mate_send.at[0], mate_recv.at[r], mate
@@ -341,8 +336,6 @@
     acc[...] = jnp.zeros_like(acc)
     mref[...] = jnp.full_like(mref, -1e30)
     ones = jnp.ones((16, 1024), BF)
-    landed(1)
-
     def logits(step, t, slot):
         keys = jnp.concatenate([kv[2 * step, 0:512, :], kv[2 * step + 1, 0:512, :]], axis=0)
         s = lax.dot_general(keys, q_buf[t], NT, preferred_element_type=F32)
@@ -372,13 +365,26 @@
             block_max, rescale = following, next_rescale
         return block_max, rescale
 
-    first = weigh(0, 0, logits(0, 0, 0))
-    state = (logits(0, 1, 1), first)
+    def q_arrive(r):
+        remote(
+            q_buf.at[3], q_buf.at[3 - r], q_send.at[0], q_recv.at[r - 1], at(dx=1)
+        ).wait_recv()
+        mate_copy(r).start()
+
+    q_arrive(1)
+    q_arrive(2)
+    landed(1)
+    bring(1)
+    first = weigh(3, 0, logits(0, 3, 0))
+    state = (logits(0, 2, 1), first)
+    q_arrive(3)
 
     def place_of(k):
         step = jnp.where(k < 4, lax.rem(k, 2), lax.div(k, 2))
-        group = jnp.where(k < 4, lax.div(k, 2), lax.rem(k, 2))
-        return step, 4 * group
+        return step, jnp.where(k < 4, lax.div(k, 2), lax.rem(k, 2))
+
+    def tile_at(group, u):
+        return jnp.where(group == 0, 3 - u, 4 + u)
 
     def by_step(k, state):
         @pl.when(k == 0)
@@ -421,12 +427,14 @@
             ready(5)
             bring(7)
 
-        step, tile = place_of(k)
-        next_step, next_tile = place_of(k + 1)
+        step, group = place_of(k)
+        next_step, next_group = place_of(k + 1)
         last = k == 7
-        units = [(step, tile + u) for u in range(4)]
-        units.append((next_step, jnp.where(last, 7, next_tile)))
-        units.append((jnp.where(last, 5, next_step), jnp.where(last, 7, next_tile + 1)))
+        units = [(step, tile_at(group, u)) for u in range(4)]
+        units.append((next_step, jnp.where(last, 7, tile_at(next_group, 0))))
+        units.append(
+            (jnp.where(last, 5, next_step), jnp.where(last, 7, tile_at(next_group, 1)))
+        )
         return turns(units, state)
 
     state = lax.fori_loop(0, 8, by_step, state)

time: 124 us -> 124 us (level)
  no operation moved by 1% of the time
where the time goes in v9:
time: 124 us; the launch traced here: 123 us
  Pallas kernels  121 us (98%)
  local copies, waits for them, and re-layouts  1.87 us (2%)
    pallas_call x1, Pallas kernels, on_device(): pl.pallas_call(kernel, out_shape=jax.ShapeDtypeStruct((ROWS, 512), BF), i...  121 us

profile of v9, /device:TPU:0, one launch (start us, length us, event | category | flops | bytes accessed | tf_op | source)
XLA Modules:
  0.0 123.3 jit_solution(6049171884004542381)
XLA Ops:
  0.0 121.5 %block.1 = bf16[512,512]{1,0:T(8,128)(2,1)} custom-call(bf16[12,512,1024]{2,1,0:T(8,128)(2,1)} %tok_hbm.1, bf16[16,1024]{1,0:T(8,128)(2,1)} %bitcast.6, bf16[1024,1024]{1,0:T(8,128)(2,1)} %vw_hbm.1, bf16[1024,2048]{1,0:T(8,128)(2,1)} %proj_hbm.1, f32[1,2048]{1,0:T(1,128)} %bitcast.7, bf16[24576,128]{1,0:T(8,128)(2,1)} %bitcast.4, bf16[512,2048]{1,0:T(8,128)(2,1)} %bitcast.5), custom_call_target="tpu_custom_call" | custom-call | tf_op jit(solution)/shard_map/block/pallas_call | solution.py:647
  121.5 1.9 %copy.9 = bf16[512,512]{1,0:T(8,128)(2,1)} copy(bf16[512,512]{1,0:T(8,128)(2,1)} %block.1) | data formatting | bytes 1048576

commit v10 on v9

--- a/solution.py
+++ b/solution.py
@@ -222,7 +222,8 @@
         block = emb[rows, :]
         center = block - jnp.mean(block, axis=1, keepdims=True)
         variance = jnp.mean(center * center, axis=1, keepdims=True)
-        normed[rows, :] = (center / jnp.sqrt(variance + 1e-05) * gain_ref[...]).astype(BF)
+        scale = 1.0 / jnp.sqrt(variance + 1e-05)
+        normed[rows, :] = (center * scale * gain_ref[...]).astype(BF)
         return 0
 
     lax.fori_loop(0, 4, norm, 0)
@@ -359,8 +360,11 @@
     def turns(units, state):
         block_max, rescale = state
         for u in range(4):
-            following = logits(*units[u + 2], u % 2)
-            next_rescale = weigh(units[u + 1][1], (u + 1) % 2, block_max)
+            following, next_rescale = block_max, rescale
+            if u + 2 < len(units):
+                following = logits(*units[u + 2], u % 2)
+            if u + 1 < len(units):
+                next_rescale = weigh(units[u + 1][1], (u + 1) % 2, block_max)
             add(*units[u], u % 2, rescale)
             block_max, rescale = following, next_rescale
         return block_max, rescale
@@ -493,11 +497,28 @@
         inner = jnp.where(lax.rem(i, 2) == 1, 6 - lax.div(i, 2), lax.div(i, 2) - 1)
         return jnp.where(i == 0, 7, jnp.where(i == 7, 3, inner))
 
+    def finish(t):
+        r = 3 - t
+        remote(
+            res_send.at[0], res_recv.at[r], rs_send.at[0], rs_recv.at[r], mate
+        ).wait_recv()
+        remote(
+            scale_send.at[0], scale_recv.at[r], ss_send.at[0], ss_recv.at[r], mate
+        ).wait_recv()
+        here, there = mref[t, 0:1, :], scale_recv[r, 0:1, :]
+        high = jnp.maximum(here, there)
+        here = jnp.exp2(here - high)
+        there = jnp.exp2(there - high) * scale_recv[r, 1:2, :]
+        inverse = 1.0 / (here * acc[t, 128:129, :] + there)
+        both = acc[t, 0:128, :] * (here * inverse)
+        both = both + res_recv[r].astype(F32) * (there * inverse)
+        block = both.T.astype(BF)
+        return block
+
     def by_tile(i, state):
         tile = tile_of(i)
-        after = tile_of(jnp.minimum(i + 1, 7))
-        units = [(4 + j, tile) for j in range(4)] + [(4, after), (5, after)]
-        state = turns(units, state)
+        after = tile_of(i + 1)
+        state = turns([(4 + j, tile) for j in range(4)] + [(4, after), (5, after)], state)
 
         @pl.when(tile >= 4)
         def _():
@@ -511,32 +532,8 @@
 
         @pl.when(tile < 4)
         def _():
-            t = tile
-            r = 3 - t
-            remote(
-                res_send.at[0], res_recv.at[r], rs_send.at[0], rs_recv.at[r], mate
-            ).wait_recv()
-            remote(
-                scale_send.at[0], scale_recv.at[r], ss_send.at[0], ss_recv.at[r], mate
-            ).wait_recv()
-            here, there = mref[tile, 0:1, :], scale_recv[r, 0:1, :]
-            high = jnp.maximum(here, there)
-            here = jnp.exp2(here - high)
-            there = jnp.exp2(there - high) * scale_recv[r, 1:2, :]
-            inverse = 1.0 / (here * acc[tile, 128:129, :] + there)
-            both = acc[tile, 0:128, :] * (here * inverse)
-            both = both + res_recv[r].astype(F32) * (there * inverse)
-            block = both.T.astype(BF)
-
-            @pl.when(t < 3)
-            def _():
-                stage[t] = block
-                ax_copy(t).start()
-
-            @pl.when(t == 3)
-            def _():
-                att[mine] = block
-                share(3)
+            stage[tile] = finish(tile)
+            ax_copy(tile).start()
 
         @pl.when(i == 4)
         def _():
@@ -551,7 +548,10 @@
 
         return state
 
-    lax.fori_loop(0, 8, by_tile, state)
+    state = lax.fori_loop(0, 7, by_tile, state)
+    turns([(4 + j, 3) for j in range(4)], state)
+    att[mine] = finish(3)
+    share(3)
 
     def branch(dz):
         zs = lax.rem(z + dz, 4)

time: 124 us -> 123 us (level)
  no operation moved by 1% of the time
where the time goes in v10:
time: 123 us
  Pallas kernels  121 us (98%)
  local copies, waits for them, and re-layouts  1.87 us (2%)
    pallas_call x1, Pallas kernels, on_device(): pl.pallas_call(kernel, out_shape=jax.ShapeDtypeStruct((ROWS, 512), BF), i...  121 us

profile of v10, /device:TPU:0, one launch (start us, length us, event | category | flops | bytes accessed | tf_op | source)
XLA Modules:
  0.0 122.9 jit_solution(6264838150864442078)
XLA Ops:
  0.0 121.0 %block.1 = bf16[512,512]{1,0:T(8,128)(2,1)} custom-call(bf16[12,512,1024]{2,1,0:T(8,128)(2,1)} %tok_hbm.1, bf16[16,1024]{1,0:T(8,128)(2,1)} %bitcast.6, bf16[1024,1024]{1,0:T(8,128)(2,1)} %vw_hbm.1, bf16[1024,2048]{1,0:T(8,128)(2,1)} %proj_hbm.1, f32[1,2048]{1,0:T(1,128)} %bitcast.7, bf16[24576,128]{1,0:T(8,128)(2,1)} %bitcast.4, bf16[512,2048]{1,0:T(8,128)(2,1)} %bitcast.5), custom_call_target="tpu_custom_call" | custom-call | tf_op jit(solution)/shard_map/block/pallas_call | solution.py:647
  121.1 1.9 %copy.9 = bf16[512,512]{1,0:T(8,128)(2,1)} copy(bf16[512,512]{1,0:T(8,128)(2,1)} %block.1) | data formatting | bytes 1048576
